TPU v7x, 512 devices: a whole 4x4x16 slice. The times are simulated.
512 devices in a mesh: rep: 8 (over x, core), fsdp: 64 (over z, y).
Axes of the slice: x: 4, y: 4, z: 16, core: 2. Of those that a mesh axis runs over, the one named last changes fastest.
Arguments:
- partials: bfloat16 [8, 16, 512, 4096], P('rep', None, 'fsdp'), may hold values from -5 to 5
- left_basis: bfloat16 [8, 64, 512, 512], P('rep', 'fsdp'), may hold values from -0.25 to 0.25
- right_basis: bfloat16 [8, 64, 512, 512], P('rep', 'fsdp'), may hold values from -0.25 to 0.25
- first_moment: bfloat16 [8, 64, 512, 512], P('rep', 'fsdp'), may hold values from -4 to 4
- second_moment: bfloat16 [8, 64, 512, 512], P('rep', 'fsdp'), may hold values from 0.099609375 to 2
- owners: int32 [8, 16], replicated, may hold values from 0 to 63, as said below
Outputs:
- first_new: bfloat16 [8, 64, 512, 512], P('rep', 'fsdp')
- second_new: bfloat16 [8, 64, 512, 512], P('rep', 'fsdp')
- update: bfloat16 [16, 512, 4096], P(None, 'fsdp', 'rep')
Inputs may be any that keep to these rules, and one draw needn't show every extreme that they name: Within each row of owners the 16 entries are distinct; each row contains 0 and 64 - 1.
All inputs are finite; a program needn't handle non-finite values.
Results may differ from a plain program's by a relative error of at most 0.015.
Values may be sent and summed in bfloat16 or wider, within the bound.
No kernel may reach another device: no remote copies, remote signals or barrier semaphores. Data moves between devices by JAX's collectives and lax.ppermute only.
A program may use at most 64 MiB of HBM per device.

v0:
```python
import jax
import jax.numpy as jnp
from jax import lax
from jax.sharding import PartitionSpec as P


def owner_selector(owner_row, fsdp_count):
    slots = jnp.arange(fsdp_count, dtype=jnp.int32)
    return (owner_row[None, :] == slots[:, None]).astype(jnp.bfloat16)


def local(partials, left_basis, right_basis, first_moment, second_moment, owners):
    fsdp_count = lax.axis_size("fsdp")
    blocks_row = partials.shape[1]
    sub_rows = partials.shape[2]
    block_side = left_basis.shape[2]
    block_count = owners.shape[1]
    col_blocks = block_count // blocks_row
    owner_row = lax.dynamic_slice_in_dim(owners, lax.axis_index("rep"), 1, 0)[0]
    selector = owner_selector(owner_row, fsdp_count)
    summed = lax.psum_scatter(
        partials.astype(jnp.float32).astype(jnp.bfloat16), "rep", scatter_dimension=3, tiled=True
    )
    pieces = summed[0].reshape(blocks_row, sub_rows, col_blocks, block_side).transpose(0, 2, 1, 3)
    pieces = pieces.reshape(block_count, sub_rows, block_side)
    outgoing = jnp.einsum(
        "qb,bsk->qsk", selector, pieces, preferred_element_type=jnp.float32
    ).astype(jnp.bfloat16)
    arrived = lax.all_to_all(outgoing, "fsdp", split_axis=0, concat_axis=0, tiled=True)
    grad_block = arrived.reshape(block_side, block_side)
    basis_left = left_basis[0, 0]
    basis_right = right_basis[0, 0]
    rotated_left = lax.dot_general(
        basis_left, grad_block, (((0,), (0,)), ((), ())), preferred_element_type=jnp.float32
    ).astype(jnp.bfloat16)
    rotated = jnp.dot(rotated_left, basis_right, preferred_element_type=jnp.float32)
    moment_one = 0.95 * first_moment[0, 0].astype(jnp.float32) + 0.05 * rotated
    moment_two = 0.95 * second_moment[0, 0].astype(jnp.float32) + 0.05 * rotated * rotated
    step_ratio = (moment_one / (jnp.sqrt(moment_two) + 1e-08)).astype(jnp.bfloat16)
    back_left = jnp.dot(basis_left, step_ratio, preferred_element_type=jnp.float32).astype(
        jnp.bfloat16
    )
    block_update = lax.dot_general(
        back_left, basis_right, (((1,), (1,)), ((), ())), preferred_element_type=jnp.float32
    ).astype(jnp.bfloat16)
    leaving = block_update.reshape(fsdp_count, sub_rows, block_side)
    returned = lax.all_to_all(leaving, "fsdp", split_axis=0, concat_axis=0, tiled=True)
    own_pieces = jnp.einsum(
        "qb,qsk->bsk", selector, returned, preferred_element_type=jnp.float32
    ).astype(jnp.bfloat16)
    update = own_pieces.reshape(blocks_row, col_blocks, sub_rows, block_side).transpose(0, 2, 1, 3)
    update = update.reshape(blocks_row, sub_rows, col_blocks * block_side)
    first_new = moment_one.astype(jnp.bfloat16)[None, None]
    second_new = moment_two.astype(jnp.bfloat16)[None, None]
    return (first_new, second_new, update)


def solution(mesh):
    return jax.shard_map(
        local,
        mesh=mesh,
        in_specs=(
            P("rep", None, "fsdp", None),
            P("rep", "fsdp", None, None),
            P("rep", "fsdp", None, None),
            P("rep", "fsdp", None, None),
            P("rep", "fsdp", None, None),
            P(),
        ),
        out_specs=(
            P("rep", "fsdp", None, None),
            P("rep", "fsdp", None, None),
            P(None, "fsdp", "rep"),
        ),
        check_vma=False,
    )
```

profile of v0, /device:TPU:6, one launch (start us, length us, event | category | flops | bytes accessed | tf_op | source)
XLA Modules:
  0.0 154.7 jit_solution(13710655851866005752)
XLA Ops:
  7.2 0.0 copy-start
  7.2 0.0 reduce-scatter.2.cloned.1.call-start
  7.2 0.7 reduce-scatter.2.cloned.1.call-update
  7.9 0.7 dynamic-slice_bitcast_fusion
  8.6 43.1 %reduce-scatter.2.cloned.1.call-done = bf16[1,16,8,512]{3,2,1,0:T(8,128)(2,1)} async-done(((bf16[1,16,8,4096]{3,2,1,0:T(8,128)(2,1)}), bf16[1,16,8,512]{3,2,1,0:T(8,128)(2,1)}) %reduce-scatter.2.cloned.1.call-update) | async-done | bytes 131088 | tf_op jit(solution)/shard_map/reduce_scatter | solution.py:21
  51.7 1.3 convolution_convert_fusion.3
  53.0 0.3 copy.17
  53.3 49.7 %all_to_all.10 = bf16[64,8,512]{2,1,0:T(8,128)(2,1)S(1)} all-to-all(bf16[64,8,512]{2,1,0:T(8,128)(2,1)S(1)} %copy.17), channel_id=1, replica_groups=mesh['rep'=8,'fsdp'=64] {'fsdp'}, dimensions={0} | all-to-all | bytes 1048576 | tf_op jit(solution)/shard_map/all_to_all | solution.py:29
  103.0 0.0 copy-done
  103.0 0.0 copy-start.1
  103.0 0.0 copy-start.2
  103.0 2.0 %fusion = f32[512,512]{1,0:T(8,128)S(1)} fusion(bf16[1,1,512,512]{3,2,1,0:T(8,128)(2,1)S(1)} %copy-done, bf16[1,1,512,512]{3,2,1,0:T(8,128)(2,1)} %param.7, bf16[64,8,512]{2,1,0:T(8,128)(2,1)S(1)} %all_to_all.10), kind=kOutput, calls=%fused_computation.6 | convolution fusion | flops 537133056 | bytes 2621440 | tf_op jit(solution)/shard_map/dot_general | solution.py:36
  105.0 0.0 copy-done.1
  105.0 0.0 copy-done.2
  105.0 3.1 %fusion.1 = bf16[64,8,512]{2,1,0:T(8,128)(2,1)} fusion(bf16[1,1,512,512]{3,2,1,0:T(8,128)(2,1)S(1)} %copy-done, bf16[1,1,512,512]{3,2,1,0:T(8,128)(2,1)} %param.7, f32[512,512]{1,0:T(8,128)S(1)} %fusion, bf16[1,1,512,512]{3,2,1,0:T(8,128)(2,1)S(1)} %copy-done.2, bf16[1,1,512,512]{3,2,1,0:T(8,128)(2,1)S(1)} %copy-done.1), kind=kOutput, calls=%fused_computation.7 | convolution fusion | flops 540278784 | bytes 3670016 | tf_op jit(solution)/shard_map/dot_general | solution.py:43
  108.1 5.7 %all-to-all-start.1 = ((bf16[64,8,512]{2,1,0:T(8,128)(2,1)}), bf16[64,8,512]{2,1,0:T(8,128)(2,1)S(1)}, u32[]{:S(2)}, u32[]{:S(2)}) async-start(bf16[64,8,512]{2,1,0:T(8,128)(2,1)} %fusion.1), calls=%async_computation.2 | async-start | bytes 1048576 | tf_op jit(solution)/shard_map/all_to_all | solution.py:47
  113.8 1.3 fusion.5
  115.1 31.8 %all-to-all-done.1 = bf16[64,8,512]{2,1,0:T(8,128)(2,1)S(1)} async-done(((bf16[64,8,512]{2,1,0:T(8,128)(2,1)}), bf16[64,8,512]{2,1,0:T(8,128)(2,1)S(1)}, u32[]{:S(2)}, u32[]{:S(2)}) %all-to-all-start.1) | async-done | bytes 524320 | tf_op jit(solution)/shard_map/all_to_all | solution.py:47
  146.9 0.3 convolution_convert_fusion.4
  147.1 0.7 copy.19
Async XLA Ops:
  7.2 95.8 %copy-start = (bf16[1,1,512,512]{3,2,1,0:T(8,128)(2,1)S(1)}, bf16[1,1,512,512]{3,2,1,0:T(8,128)(2,1)}, u32[]{:S(2)}) copy-start(bf16[1,1,512,512]{3,2,1,0:T(8,128)(2,1)} %param.8) | copy-start | bytes 1572868
  7.2 44.5 %reduce-scatter.2.cloned.1.call-start = ((), (), s32[]{:S(2)}) async-start(), calls=%async_computation.3 | async-start | bytes 1179648 | tf_op jit(solution)/shard_map/reduce_scatter | solution.py:21
  103.0 2.0 %copy-start.1 = (bf16[1,1,512,512]{3,2,1,0:T(8,128)(2,1)S(1)}, bf16[1,1,512,512]{3,2,1,0:T(8,128)(2,1)}, u32[]{:S(2)}) copy-start(bf16[1,1,512,512]{3,2,1,0:T(8,128)(2,1)} %param.10) | copy-start | bytes 1572868
  103.0 2.0 %copy-start.2 = (bf16[1,1,512,512]{3,2,1,0:T(8,128)(2,1)S(1)}, bf16[1,1,512,512]{3,2,1,0:T(8,128)(2,1)}, u32[]{:S(2)}) copy-start(bf16[1,1,512,512]{3,2,1,0:T(8,128)(2,1)} %param.9) | copy-start | bytes 1572868
  108.1 38.8 %all-to-all-start.1 = ((bf16[64,8,512]{2,1,0:T(8,128)(2,1)}), bf16[64,8,512]{2,1,0:T(8,128)(2,1)S(1)}, u32[]{:S(2)}, u32[]{:S(2)}) async-start(bf16[64,8,512]{2,1,0:T(8,128)(2,1)} %fusion.1), calls=%async_computation.2 | async-start | bytes 1048576 | tf_op jit(solution)/shard_map/all_to_all | solution.py:47
Sparse Core Ops, SparseCore 0:
  10.8 40.8 reduce-scatter.1
where the time goes:
time: 155 us
  waiting for transfers between devices  75.5 us (49%)
  blocking collectives  49.7 us (32%)
  between operations  14.1 us (9%)
  matrix products  6.67 us (4%)
  starting transfers between devices  5.7 us (4%)
  local copies, waits for them, and re-layouts  1.74 us (1%)
    all_to_all x1, blocking collectives, local(): lax.all_to_all(outgoing, 'fsdp', split_axis=0, concat_axis=0, tiled=True)  49.7 us
    reduce_scatter x1, waiting for transfers between devices, local(): lax.psum_scatter(partials.astype(jnp.float32).astype(jnp.bfloat16), 'rep'...  43.1 us
    all_to_all x1, waiting for transfers between devices, local(): lax.all_to_all(leaving, 'fsdp', split_axis=0, concat_axis=0, tiled=True)  31.8 us
    all_to_all x1, starting transfers between devices, local(): lax.all_to_all(leaving, 'fsdp', split_axis=0, concat_axis=0, tiled=True)  5.66 us
  transfers between devices with their start and end apart: 2, of which 2 were waited for; matrix products, arithmetic and copies ran while one was open for 1% of the time, Pallas kernels for 0%

commit v1 on v0

v1 whole, which is shorter than its diff:
```python
import jax
import jax.numpy as jnp
from jax import lax
from jax.experimental import pallas as pl
from jax.experimental.pallas import tpu as pltpu
from jax.sharding import PartitionSpec as P

N_REP = 8
N_FSDP = 64
SUB = 8
SIDE = 512
BLOCKS = 16
STRIP = 128

FIRST = N_FSDP // 2
ORDER = [(p + FIRST) % N_FSDP for p in range(N_FSDP)]


def hbm():
    return pl.BlockSpec(memory_space=pl.ANY)


def vmem():
    return pl.BlockSpec(memory_space=pltpu.VMEM)


def cut_kernel(partials, blocks, held, in_sems, out_sems):
    loads = [
        pltpu.make_async_copy(
            partials.at[0, :, :, pl.ds(r * SIDE, SIDE)], held.at[r], in_sems.at[r]
        )
        for r in range(N_REP)
    ]
    stores = [
        pltpu.make_async_copy(held.at[r], blocks.at[r], out_sems.at[r]) for r in range(N_REP)
    ]
    for c in loads:
        c.start()
    for load, store in zip(loads, stores):
        load.wait()
        store.start()
    for c in stores:
        c.wait()


def cut_columns(partials):
    shape = (N_REP, BLOCKS, SUB, SIDE)
    return pl.pallas_call(
        cut_kernel,
        out_shape=jax.ShapeDtypeStruct(shape, jnp.bfloat16),
        in_specs=[hbm()],
        out_specs=hbm(),
        scratch_shapes=[
            pltpu.VMEM(shape, jnp.bfloat16),
            pltpu.SemaphoreType.DMA((N_REP,)),
            pltpu.SemaphoreType.DMA((N_REP,)),
        ],
        name="cut_columns",
    )(partials)


def step_kernel(
    grad, left, left_turned, right, right_turned, first, second,
    first_new_hbm, second_new_hbm, block_update,
    first_new, second_new, ratio, sems,
):
    turned = jnp.dot(left_turned[...], grad[...], preferred_element_type=jnp.float32).astype(
        jnp.bfloat16
    )
    for i in range(SIDE // STRIP):
        rows = slice(i * STRIP, (i + 1) * STRIP)
        rotated = jnp.dot(turned[rows], right[...], preferred_element_type=jnp.float32)
        one = 0.95 * first[rows, :].astype(jnp.float32) + 0.05 * rotated
        two = 0.95 * second[rows, :].astype(jnp.float32) + 0.05 * rotated * rotated
        first_new[rows, :] = one.astype(jnp.bfloat16)
        second_new[rows, :] = two.astype(jnp.bfloat16)
        ratio[rows, :] = (one / (jnp.sqrt(two) + 1e-08)).astype(jnp.bfloat16)
    stores = [
        pltpu.make_async_copy(first_new, first_new_hbm, sems.at[0]),
        pltpu.make_async_copy(second_new, second_new_hbm, sems.at[1]),
    ]
    for c in stores:
        c.start()
    back = jnp.dot(left[...], ratio[...], preferred_element_type=jnp.float32).astype(jnp.bfloat16)
    block_update[...] = jnp.dot(
        back, right_turned[...], preferred_element_type=jnp.float32
    ).astype(jnp.bfloat16)
    for c in stores:
        c.wait()


def step(*operands):
    square = jax.ShapeDtypeStruct((SIDE, SIDE), jnp.bfloat16)
    return pl.pallas_call(
        step_kernel,
        out_shape=(square, square, square),
        in_specs=[vmem()] * 7,
        out_specs=(hbm(), hbm(), vmem()),
        scratch_shapes=[pltpu.VMEM((SIDE, SIDE), jnp.bfloat16)] * 3 + [pltpu.SemaphoreType.DMA((2,))],
        compiler_params=pltpu.CompilerParams(vmem_limit_bytes=24 * 1024 * 1024),
        cost_estimate=pl.CostEstimate(
            flops=8 * SIDE**3, bytes_accessed=18 * SIDE**2, transcendentals=2 * SIDE**2
        ),
        name="soap_step",
    )(*operands)


def exchange(pieces):
    return lax.all_to_all(pieces, "fsdp", 0, 0, axis_index_groups=[ORDER], tiled=True)


def local(partials, left_basis, right_basis, first_moment, second_moment, owners):
    owner_row = lax.dynamic_slice_in_dim(owners, lax.axis_index("rep"), 1, 0)[0]
    places = lax.rem(owner_row + (N_FSDP - FIRST), N_FSDP)
    slots = jnp.arange(N_FSDP, dtype=jnp.int32)
    selector = (places[None, :] == slots[:, None]).astype(jnp.bfloat16)

    parts = lax.all_to_all(cut_columns(partials), "rep", 0, 0, tiled=True)
    right = right_basis[0, 0]
    left = jnp.roll(left_basis[0, 0], -FIRST * SUB, 0)
    parts, left, left_turned, right_turned, selector = lax.optimization_barrier(
        (parts, left, left.T, right.T, selector)
    )
    pieces = jnp.sum(parts.astype(jnp.float32), axis=0).astype(jnp.bfloat16)
    outgoing = jnp.einsum(
        "qb,bsk->qsk", selector, pieces, preferred_element_type=jnp.float32
    ).astype(jnp.bfloat16)
    arrived = exchange(outgoing)
    first_new, second_new, block_update = step(
        arrived.reshape(SIDE, SIDE), left, left_turned, right, right_turned,
        first_moment[0, 0], second_moment[0, 0],
    )
    returned = exchange(block_update.reshape(N_FSDP, SUB, SIDE))
    update = jnp.einsum(
        "qb,qsk->bsk", selector, returned, preferred_element_type=jnp.float32
    ).astype(jnp.bfloat16)
    return (first_new[None, None], second_new[None, None], update)


def solution(mesh):
    return jax.shard_map(
        local,
        mesh=mesh,
        in_specs=(
            P("rep", None, "fsdp", None),
            P("rep", "fsdp", None, None),
            P("rep", "fsdp", None, None),
            P("rep", "fsdp", None, None),
            P("rep", "fsdp", None, None),
            P(),
        ),
        out_specs=(
            P("rep", "fsdp", None, None),
            P("rep", "fsdp", None, None),
            P(None, "fsdp", "rep"),
        ),
        check_vma=False,
    )
```

time: 155 us -> 113 us (0.73)
  waiting for transfers between devices: 75.5 us -> 34.6 us
  starting transfers between devices: 5.7 us -> 27.1 us
  between operations: 14.1 us -> 0.73 us
  blocking collectives: 49.7 us -> 37.6 us
  matrix products: 6.67 us -> 0.59 us
  Pallas kernels: 0 us -> 4.3 us
  local copies, waits for them, and re-layouts: 1.74 us -> 5.45 us
    reduce_scatter x1 -> x0, waiting for transfers between devices: 43.1 us -> none  [local(): lax.psum_scatter(partials.astype(jnp.float32).astype(jnp.bfloat16), 'rep'...]
    all_to_all x1 -> x2, starting transfers between devices: 5.66 us -> 27.1 us  [the longest x1 17.6 us: exchange(): lax.all_to_all(pieces, 'fsdp', 0, 0, axis_index_groups=[ORDER], tiled=True)]
    all_to_all x1, blocking collectives: 49.7 us -> 37.6 us  [exchange(): lax.all_to_all(pieces, 'fsdp', 0, 0, axis_index_groups=[ORDER], tiled=True)]
    dot_general x2 -> x0, matrix products: 5.09 us -> none  [the longest x1 3.09 us: local(): lax.dot_general(back_left, basis_right, (((1,), (1,)), ((), ())), preferr...]
    pallas_call x0 -> x2, Pallas kernels: none -> 4.3 us  [the longest x1 2.19 us: step(): pl.pallas_call(step_kernel, out_shape=(square, square, square), in_specs=...]
    all_to_all x1 -> x2, waiting for transfers between devices: 31.8 us -> 34.6 us  [the longest x1 23.7 us: exchange(): lax.all_to_all(pieces, 'fsdp', 0, 0, axis_index_groups=[ORDER], tiled=True)]
    unnamed x7 -> x12, local copies, waits for them, and re-layouts: 0.75 us -> 3.02 us
  transfers between devices with their start and end apart: 2 -> 2, of which waited for: 2 -> 2; matrix products, arithmetic and copies ran while one was open for 1% -> 3% of each run, Pallas kernels for 0% -> 0%
where the time goes in v1:
time: 113 us; the launch traced here: 112 us
  blocking collectives  37.6 us (33%)
  waiting for transfers between devices  34.6 us (31%)
  starting transfers between devices  27.1 us (24%)
  local copies, waits for them, and re-layouts  5.45 us (5%)
  Pallas kernels  4.3 us (4%)
  other arithmetic  1.79 us (2%)
    all_to_all x1, blocking collectives, exchange(): lax.all_to_all(pieces, 'fsdp', 0, 0, axis_index_groups=[ORDER], tiled=True)  37.6 us
    all_to_all x1, waiting for transfers between devices, exchange(): lax.all_to_all(pieces, 'fsdp', 0, 0, axis_index_groups=[ORDER], tiled=True)  23.7 us
    all_to_all x1, starting transfers between devices, exchange(): lax.all_to_all(pieces, 'fsdp', 0, 0, axis_index_groups=[ORDER], tiled=True)  17.6 us
    all_to_all x1, waiting for transfers between devices, local(): parts = lax.all_to_all(cut_columns(partials), 'rep', 0, 0, tiled=True)  10.9 us
    all_to_all x1, starting transfers between devices, local(): parts = lax.all_to_all(cut_columns(partials), 'rep', 0, 0, tiled=True)  9.49 us
    unnamed x12, local copies, waits for them, and re-layouts  3.02 us
  transfers between devices with their start and end apart: 2, of which 2 were waited for; matrix products, arithmetic and copies ran while one was open for 3% of the time, Pallas kernels for 0%

profile of v1, /device:TPU:6, one launch (start us, length us, event | category | flops | bytes accessed | tf_op | source)
XLA Modules:
  0.0 112.1 jit_solution(4217274551613006458)
XLA Ops:
  0.6 2.1 %cut_columns.1 = bf16[8,16,8,512]{3,2,1,0:T(8,128)(2,1)} custom-call(bf16[1,16,8,4096]{3,2,1,0:T(8,128)(2,1)} %partials.1), custom_call_target="tpu_custom_call" | custom-call | tf_op jit(solution)/shard_map/cut_columns/pallas_call | solution.py:48
  2.7 0.0 copy-start.3
  2.8 9.5 %all-to-all-start = ((bf16[8,16,8,512]{3,2,1,0:T(8,128)(2,1)}), bf16[8,16,8,512]{3,2,1,0:T(8,128)(2,1)S(1)}, u32[]{:S(2)}, u32[]{:S(2)}) async-start(bf16[8,16,8,512]{3,2,1,0:T(8,128)(2,1)} %cut_columns.1), calls=%async_computation | async-start | bytes 2097152 | tf_op jit(solution)/shard_map/all_to_all | solution.py:118
  12.3 0.0 copy-start
  12.3 0.1 copy.27
  12.4 0.1 copy.28
  12.6 0.8 copy-done
  13.3 0.2 copy.19
  13.5 0.7 fusion.6
  14.3 0.9 fusion.7
  15.1 0.1 fusion.2
  15.2 10.9 %all-to-all-done = bf16[8,16,8,512]{3,2,1,0:T(8,128)(2,1)S(1)} async-done(((bf16[8,16,8,512]{3,2,1,0:T(8,128)(2,1)}), bf16[8,16,8,512]{3,2,1,0:T(8,128)(2,1)S(1)}, u32[]{:S(2)}, u32[]{:S(2)}) %all-to-all-start) | async-done | bytes 1048608 | tf_op jit(solution)/shard_map/all_to_all | solution.py:118
  26.1 0.1 reduce_sum.12
  26.3 0.3 convolution_convert_fusion
  26.6 1.1 copy.21
  27.7 17.6 %all-to-all-start.1 = ((bf16[64,8,512]{2,1,0:T(8,128)(2,1)}), bf16[64,8,512]{2,1,0:T(8,128)(2,1)S(1)}, u32[]{:S(2)}, u32[]{:S(2)}) async-start(bf16[64,8,512]{2,1,0:T(8,128)(2,1)} %copy.21), calls=%async_computation.1 | async-start | bytes 1048576 | tf_op jit(solution)/shard_map/all_to_all | solution.py:109
  45.3 0.0 copy-start.1
  45.3 1.3 %copy.22.left = bf16[512,512]{1,0:T(8,128)(2,1)S(1)} copy(bf16[512,512]{0,1:T(8,128)(2,1)} %get-tuple-element.13) | data formatting | bytes 1048576 | tf_op jit(solution)/shard_map/optimization_barrier | solution.py:121
  46.6 23.7 %all-to-all-done.1 = bf16[64,8,512]{2,1,0:T(8,128)(2,1)S(1)} async-done(((bf16[64,8,512]{2,1,0:T(8,128)(2,1)}), bf16[64,8,512]{2,1,0:T(8,128)(2,1)S(1)}, u32[]{:S(2)}, u32[]{:S(2)}) %all-to-all-start.1) | async-done | bytes 524320 | tf_op jit(solution)/shard_map/all_to_all | solution.py:109
  70.3 1.0 copy-done.2
  71.3 2.2 %soap_step.1 = (bf16[512,512]{1,0:T(8,128)(2,1)}, bf16[512,512]{1,0:T(8,128)(2,1)}, bf16[512,512]{1,0:T(8,128)(2,1)S(1)}) custom-call(bf16[512,512]{1,0:T(8,128)(2,1)S(1)} %bitcast.23, bf16[512,512]{1,0:T(8,128)(2,1)S(1)} %copy.22.left, bf16[512,512]{1,0:T(8,128)(2,1)S(1)} %get-tuple-element.14.left_turned, bf16[512,512]{1,0:T(8,128)(2,1)S(1)} %bitcast.21, ...), custom_call_target="tpu_custom_call" | custom-call | flops 1073741824 | bytes 4718592 | tf_op jit(solution)/shard_map/soap_step/pallas_call | solution.py:94
  73.5 37.6 %all_to_all.15 = bf16[64,8,512]{2,1,0:T(8,128)(2,1)S(1)} all-to-all(bf16[64,8,512]{2,1,0:T(8,128)(2,1)S(1)} %bitcast.24), channel_id=1, replica_groups={{32,33,34,35,36,37,38,39,40,41,42,43,44,45,46,47,48,49,50,51,52,53,54,5..., dimensions={0} | all-to-all | bytes 1048576 | tf_op jit(solution)/shard_map/all_to_all | solution.py:109
  111.1 0.3 convolution_convert_fusion.1
  111.4 0.7 copy.25
  (4 shorter events, 0.0 us)
Async XLA Ops:
  2.7 9.5 %copy-start.3 = (bf16[1,1,512,512]{3,2,1,0:T(8,128)(2,1)S(1)}, bf16[1,1,512,512]{3,2,1,0:T(8,128)(2,1)}, u32[]{:S(2)}) copy-start(bf16[1,1,512,512]{3,2,1,0:T(8,128)(2,1)} %param.7) | copy-start | bytes 1572868
  2.8 23.4 %all-to-all-start = ((bf16[8,16,8,512]{3,2,1,0:T(8,128)(2,1)}), bf16[8,16,8,512]{3,2,1,0:T(8,128)(2,1)S(1)}, u32[]{:S(2)}, u32[]{:S(2)}) async-start(bf16[8,16,8,512]{3,2,1,0:T(8,128)(2,1)} %cut_columns.1), calls=%async_computation | async-start | bytes 2097152 | tf_op jit(solution)/shard_map/all_to_all | solution.py:118
  12.3 1.0 copy-start
  27.7 42.6 %all-to-all-start.1 = ((bf16[64,8,512]{2,1,0:T(8,128)(2,1)}), bf16[64,8,512]{2,1,0:T(8,128)(2,1)S(1)}, u32[]{:S(2)}, u32[]{:S(2)}) async-start(bf16[64,8,512]{2,1,0:T(8,128)(2,1)} %copy.21), calls=%async_computation.1 | async-start | bytes 1048576 | tf_op jit(solution)/shard_map/all_to_all | solution.py:109
  45.3 25.0 %copy-start.1 = (bf16[1,1,512,512]{3,2,1,0:T(8,128)(2,1)S(1)}, bf16[1,1,512,512]{3,2,1,0:T(8,128)(2,1)}, u32[]{:S(2)}) copy-start(bf16[1,1,512,512]{3,2,1,0:T(8,128)(2,1)} %param.9) | copy-start | bytes 1572868
  70.3 1.0 copy-start.2

commit v2 on v1

v2 whole, which is shorter than its diff:
```python
import jax
import jax.numpy as jnp
from jax import lax
from jax.experimental import pallas as pl
from jax.experimental.pallas import tpu as pltpu
from jax.sharding import PartitionSpec as P

N_X = 4
N_Y = 4
N_Z = 16
N_FSDP = N_Z * N_Y
SUB = 8
SIDE = 512
BLOCKS = 16
STRIP = 128

PLANES = [8, 0, 1, 15, 2, 14, 3, 13, 4, 12, 5, 11, 6, 10, 7, 9]
ORDER = [z * N_Y + (y + N_Y // 2) % N_Y for z in PLANES for y in range(N_Y)]
PAIR = 2 * SUB


def chip_of(p):
    return (p + N_X // 2) % N_X


def hbm():
    return pl.BlockSpec(memory_space=pl.ANY)


def vmem():
    return pl.BlockSpec(memory_space=pltpu.VMEM)


def pair_kernel(own, other, pair):
    core = lax.rem(lax.axis_index("rep"), 2)
    for p in range(N_X):
        columns = pl.ds(pl.multiple_of((2 * chip_of(p) + core) * SIDE, SIDE), SIDE)
        total = own[:, :, columns].astype(jnp.float32) + other[:, :, columns].astype(jnp.float32)
        pair[p] = total.astype(jnp.bfloat16)


def add_pair(own, other):
    return pl.pallas_call(
        pair_kernel,
        out_shape=jax.ShapeDtypeStruct((N_X, BLOCKS, SUB, SIDE), jnp.bfloat16),
        in_specs=[vmem(), vmem()],
        out_specs=vmem(),
        compiler_params=pltpu.CompilerParams(vmem_limit_bytes=16 * 1024 * 1024),
        name="add_pair",
    )(own, other)


def step_kernel(
    arrived, left, left_turned, right, right_turned, first, second,
    first_new_hbm, second_new_hbm, leaving,
    grad, first_new, second_new, ratio, sems,
):
    places = [
        (slice(p * SUB, p * SUB + PAIR), slice(ORDER[p] * SUB, ORDER[p] * SUB + PAIR))
        for p in range(0, N_FSDP, 2)
    ]
    for here, natural in places:
        grad[natural, :] = arrived[here, :]
    turned = jnp.dot(left_turned[...], grad[...], preferred_element_type=jnp.float32).astype(
        jnp.bfloat16
    )
    for i in range(SIDE // STRIP):
        rows = slice(i * STRIP, (i + 1) * STRIP)
        rotated = jnp.dot(turned[rows], right[...], preferred_element_type=jnp.float32)
        one = 0.95 * first[rows, :].astype(jnp.float32) + 0.05 * rotated
        two = 0.95 * second[rows, :].astype(jnp.float32) + 0.05 * rotated * rotated
        first_new[rows, :] = one.astype(jnp.bfloat16)
        second_new[rows, :] = two.astype(jnp.bfloat16)
        ratio[rows, :] = (one / (jnp.sqrt(two) + 1e-08)).astype(jnp.bfloat16)
    stores = [
        pltpu.make_async_copy(first_new, first_new_hbm, sems.at[0]),
        pltpu.make_async_copy(second_new, second_new_hbm, sems.at[1]),
    ]
    for c in stores:
        c.start()
    back = jnp.dot(left[...], ratio[...], preferred_element_type=jnp.float32).astype(jnp.bfloat16)
    block_update = jnp.dot(back, right_turned[...], preferred_element_type=jnp.float32).astype(
        jnp.bfloat16
    )
    for here, natural in places:
        leaving[here, :] = block_update[natural, :]
    for c in stores:
        c.wait()


def step(*operands):
    square = jax.ShapeDtypeStruct((SIDE, SIDE), jnp.bfloat16)
    return pl.pallas_call(
        step_kernel,
        out_shape=(square, square, square),
        in_specs=[vmem()] * 7,
        out_specs=(hbm(), hbm(), vmem()),
        scratch_shapes=[pltpu.VMEM((SIDE, SIDE), jnp.bfloat16)] * 4 + [pltpu.SemaphoreType.DMA((2,))],
        compiler_params=pltpu.CompilerParams(vmem_limit_bytes=24 * 1024 * 1024),
        cost_estimate=pl.CostEstimate(
            flops=8 * SIDE**3, bytes_accessed=18 * SIDE**2, transcendentals=2 * SIDE**2
        ),
        name="soap_step",
    )(*operands)


def exchange(pieces):
    return lax.all_to_all(pieces, "fsdp", 0, 0, axis_index_groups=[ORDER], tiled=True)


def local(partials, left_basis, right_basis, first_moment, second_moment, owners):
    owner_row = lax.dynamic_slice_in_dim(owners, lax.axis_index("rep"), 1, 0)[0]
    slots = jnp.array(ORDER, jnp.int32)
    selector = (owner_row[None, :] == slots[:, None]).astype(jnp.bfloat16)
    left = left_basis[0, 0]
    right = right_basis[0, 0]

    own = partials[0]
    other = lax.ppermute(own, "rep", [(i, i ^ 1) for i in range(2 * N_X)])
    other, left_turned, right_turned, selector = lax.optimization_barrier(
        (other, left.T, right.T, selector)
    )
    pair = add_pair(own, other)
    chips = [[2 * chip_of(p) + core for p in range(N_X)] for core in range(2)]
    parts = lax.all_to_all(pair, "rep", 0, 0, axis_index_groups=chips, tiled=True)
    pieces = jnp.sum(parts.astype(jnp.float32), axis=0).astype(jnp.bfloat16)

    outgoing = jnp.einsum(
        "qb,bsk->qsk", selector, pieces, preferred_element_type=jnp.float32
    ).astype(jnp.bfloat16)
    arrived = exchange(outgoing)
    first_new, second_new, leaving = step(
        arrived.reshape(SIDE, SIDE), left, left_turned, right, right_turned,
        first_moment[0, 0], second_moment[0, 0],
    )
    returned = exchange(leaving.reshape(N_FSDP, SUB, SIDE))
    update = jnp.einsum(
        "qb,qsk->bsk", selector, returned, preferred_element_type=jnp.float32
    ).astype(jnp.bfloat16)
    return (first_new[None, None], second_new[None, None], update)


def solution(mesh):
    return jax.shard_map(
        local,
        mesh=mesh,
        in_specs=(
            P("rep", None, "fsdp", None),
            P("rep", "fsdp", None, None),
            P("rep", "fsdp", None, None),
            P("rep", "fsdp", None, None),
            P("rep", "fsdp", None, None),
            P(),
        ),
        out_specs=(
            P("rep", "fsdp", None, None),
            P("rep", "fsdp", None, None),
            P(None, "fsdp", "rep"),
        ),
        check_vma=False,
    )
```

time: 113 us -> 106 us (0.938)
  blocking collectives: 37.6 us -> 95.9 us
  waiting for transfers between devices: 34.6 us -> 0.01 us
  starting transfers between devices: 27.1 us -> 1.92 us
  Pallas kernels: 4.3 us -> 2.37 us
  other arithmetic: 1.79 us -> 0.15 us
  local copies, waits for them, and re-layouts: 5.45 us -> 4.1 us
    all_to_all x1 -> x2, blocking collectives: 37.6 us -> 79.1 us  [exchange(): lax.all_to_all(pieces, 'fsdp', 0, 0, axis_index_groups=[ORDER], tiled=True)]
    all_to_all x2 -> x0, waiting for transfers between devices: 34.6 us -> none  [the longest x1 23.7 us: exchange(): lax.all_to_all(pieces, 'fsdp', 0, 0, axis_index_groups=[ORDER], tiled=True)]
    all_to_all x2 -> x0, starting transfers between devices: 27.1 us -> none  [the longest x1 17.6 us: exchange(): lax.all_to_all(pieces, 'fsdp', 0, 0, axis_index_groups=[ORDER], tiled=True)]
    all_to_all x0 -> x1, blocking collectives: none -> 16.8 us  [local(): lax.all_to_all(pair, 'rep', 0, 0, axis_index_groups=chips, tiled=True)]
    pallas_call x1, Pallas kernels: 2.11 us -> 0.14 us  [add_pair(): pl.pallas_call(pair_kernel, out_shape=jax.ShapeDtypeStruct((N_X, BLOCKS,...]
    ppermute x0 -> x1, starting transfers between devices: none -> 1.92 us  [local(): other = lax.ppermute(own, 'rep', [(i, i ^ 1) for i in range(2 * N_X)])]
    optimization_barrier x1 -> x0, local copies, waits for them, and re-layouts: 1.31 us -> none  [local(): lax.optimization_barrier((parts, left, left.T, right.T, selector))]
    unnamed x12 -> x19, local copies, waits for them, and re-layouts: 3.02 us -> 3.8 us
  transfers between devices with their start and end apart: 2 -> 1, of which waited for: 2 -> 0; matrix products, arithmetic and copies ran while one was open for 3% -> 2% of each run, Pallas kernels for 0% -> 0%
where the time goes in v2:
time: 106 us
  blocking collectives  95.9 us (90%)
  local copies, waits for them, and re-layouts  4.1 us (4%)
  Pallas kernels  2.37 us (2%)
  starting transfers between devices  1.92 us (2%)
    all_to_all x2, blocking collectives, exchange(): lax.all_to_all(pieces, 'fsdp', 0, 0, axis_index_groups=[ORDER], tiled=True)  79.1 us
    all_to_all x1, blocking collectives, local(): lax.all_to_all(pair, 'rep', 0, 0, axis_index_groups=chips, tiled=True)  16.8 us
    unnamed x19, local copies, waits for them, and re-layouts  3.8 us
    pallas_call x1, Pallas kernels, step(): pl.pallas_call(step_kernel, out_shape=(square, square, square), in_specs=...  2.23 us
  transfers between devices with their start and end apart: 1, of which 0 were waited for; matrix products, arithmetic and copies ran while one was open for 2% of the time, Pallas kernels for 0%

profile of v2, /device:TPU:6, one launch (start us, length us, event | category | flops | bytes accessed | tf_op | source)
XLA Modules:
  0.0 105.8 jit_solution(14422406727440713408)
XLA Ops:
  0.6 0.0 copy-start
  0.6 1.9 %collective-permute-start = (bf16[16,8,4096]{2,1,0:T(8,128)(2,1)}, bf16[16,8,4096]{2,1,0:T(8,128)(2,1)S(1)}, u32[]{:S(2)}, u32[]{:S(2)}) collective-permute-start(bf16[16,8,4096]{2,1,0:T(8,128)(2,1)} %bitcast.22), channel_id=1, source_target_pairs={{0,64},{64,0},{128,192},{192,128},{256,320},{320,256},{384,448},{4... | collective-permute-start | bytes 3145736 | tf_op jit(solution)/shard_map/ppermute | solution.py:119
  2.6 0.0 copy-start.3
  2.6 1.4 %copy.17 = bf16[1,1,512,512]{2,3,1,0:T(8,128)(2,1)S(1)} copy(bf16[1,1,512,512]{3,2,1,0:T(8,128)(2,1)} %param.8) | data formatting | bytes 1048576 | tf_op args[1]
  4.0 0.0 copy-done.3
  4.0 1.0 copy.18
  5.0 0.6 copy-done.7
  5.6 0.1 compare_convert_fusion
  5.7 0.0 collective-permute-done.other
  5.7 0.1 add_pair.1
  5.9 16.8 %all_to_all.15 = bf16[4,16,8,512]{3,2,1,0:T(8,128)(2,1)S(1)} all-to-all(bf16[4,16,8,512]{3,2,1,0:T(8,128)(2,1)S(1)} %add_pair.1), channel_id=1, replica_groups={{256,384,0,128},{320,448,64,192},{257,385,1,129},{321,449,65,193},{258,..., dimensions={0} | all-to-all | bytes 1048576 | tf_op jit(solution)/shard_map/all_to_all | solution.py:125
  22.7 0.1 reduce_sum.12
  22.8 0.3 convolution_convert_fusion
  23.1 0.0 copy-start.5
  23.1 0.0 copy-start.6
  23.1 0.3 copy.20
  23.4 0.0 copy-start.2
  23.4 0.0 copy-start.4
  23.4 41.5 %all_to_all.16 = bf16[64,8,512]{2,1,0:T(8,128)(2,1)S(1)} all-to-all(bf16[64,8,512]{2,1,0:T(8,128)(2,1)S(1)} %copy.20), channel_id=1, replica_groups={{34,35,32,33,2,3,0,1,6,7,4,5,62,63,60,61,10,11,8,9,58,59,56,57,14,15,12..., dimensions={0} | all-to-all | bytes 1048576 | tf_op jit(solution)/shard_map/all_to_all | solution.py:108
  65.0 0.0 copy-done.6
  65.0 2.2 %soap_step.1 = (bf16[512,512]{1,0:T(8,128)(2,1)}, bf16[512,512]{1,0:T(8,128)(2,1)}, bf16[512,512]{1,0:T(8,128)(2,1)S(1)}) custom-call(bf16[512,512]{1,0:T(8,128)(2,1)S(1)} %bitcast.28, bf16[512,512]{1,0:T(8,128)(2,1)S(1)} %bitcast.24, bf16[512,512]{1,0:T(8,128)(2,1)S(1)} %bitcast.26, bf16[512,512]{1,0:T(8,128)(2,1)S(1)} %bitcast.25, ...), custom_call_target="tpu_custom_call" | custom-call | flops 1073741824 | bytes 4718592 | tf_op jit(solution)/shard_map/soap_step/pallas_call | solution.py:93
  67.2 37.5 %all_to_all.17 = bf16[64,8,512]{2,1,0:T(8,128)(2,1)S(1)} all-to-all(bf16[64,8,512]{2,1,0:T(8,128)(2,1)S(1)} %bitcast.29), channel_id=1, replica_groups={{34,35,32,33,2,3,0,1,6,7,4,5,62,63,60,61,10,11,8,9,58,59,56,57,14,15,12..., dimensions={0} | all-to-all | bytes 1048576 | tf_op jit(solution)/shard_map/all_to_all | solution.py:108
  104.8 0.3 convolution_convert_fusion.1
  105.1 0.7 copy.24
  (8 shorter events, 0.0 us)
Async XLA Ops:
  0.6 4.4 %copy-start = (s32[8,16]{1,0:T(8,128)S(1)}, s32[8,16]{1,0:T(8,128)}, u32[]{:S(2)}) copy-start(s32[8,16]{1,0:T(8,128)} %param.12) | copy-start | bytes 1540
  0.6 5.1 %collective-permute-start = (bf16[16,8,4096]{2,1,0:T(8,128)(2,1)}, bf16[16,8,4096]{2,1,0:T(8,128)(2,1)S(1)}, u32[]{:S(2)}, u32[]{:S(2)}) collective-permute-start(bf16[16,8,4096]{2,1,0:T(8,128)(2,1)} %bitcast.22), channel_id=1, source_target_pairs={{0,64},{64,0},{128,192},{192,128},{256,320},{320,256},{384,448},{4... | collective-permute-start | bytes 3145736 | tf_op jit(solution)/shard_map/ppermute | solution.py:119
  2.6 1.4 %copy-start.3 = (bf16[1,1,512,512]{3,2,1,0:T(8,128)(2,1)S(1)}, bf16[1,1,512,512]{3,2,1,0:T(8,128)(2,1)}, u32[]{:S(2)}) copy-start(bf16[1,1,512,512]{3,2,1,0:T(8,128)(2,1)} %param.9) | copy-start | bytes 1572868
  2.6 3.1 %copy-start.1 = (bf16[1,16,8,4096]{3,2,1,0:T(8,128)(2,1)S(1)}, bf16[1,16,8,4096]{3,2,1,0:T(8,128)(2,1)}, u32[]{:S(2)}) copy-start(bf16[1,16,8,4096]{3,2,1,0:T(8,128)(2,1)} %param.7) | copy-start | bytes 3145732
  5.0 0.7 copy-start.7
  23.1 41.9 %copy-start.5 = (bf16[1,1,512,512]{3,2,1,0:T(8,128)(2,1)S(1)}, bf16[1,1,512,512]{3,2,1,0:T(8,128)(2,1)}, u32[]{:S(2)}) copy-start(bf16[1,1,512,512]{3,2,1,0:T(8,128)(2,1)} %param.10) | copy-start | bytes 1572868
  23.1 41.9 %copy-start.6 = (bf16[1,1,512,512]{3,2,1,0:T(8,128)(2,1)S(1)}, bf16[1,1,512,512]{3,2,1,0:T(8,128)(2,1)}, u32[]{:S(2)}) copy-start(bf16[1,1,512,512]{3,2,1,0:T(8,128)(2,1)} %param.11) | copy-start | bytes 1572868
  23.4 41.6 %copy-start.2 = (bf16[1,1,512,512]{3,2,1,0:T(8,128)(2,1)S(1)}, bf16[1,1,512,512]{3,2,1,0:T(8,128)(2,1)}, u32[]{:S(2)}) copy-start(bf16[1,1,512,512]{3,2,1,0:T(8,128)(2,1)} %param.8) | copy-start | bytes 1572868
  23.4 41.5 %copy-start.4 = (bf16[1,1,512,512]{2,3,1,0:T(8,128)(2,1)S(1)}, bf16[1,1,512,512]{2,3,1,0:T(8,128)(2,1)}, u32[]{:S(2)}) copy-start(bf16[1,1,512,512]{2,3,1,0:T(8,128)(2,1)} %copy.18) | copy-start | bytes 1572868

commit v3 on v2

--- a/solution.py
+++ b/solution.py
@@ -14,15 +14,18 @@
 BLOCKS = 16
 STRIP = 128
 
-PLANES = [8, 0, 1, 15, 2, 14, 3, 13, 4, 12, 5, 11, 6, 10, 7, 9]
-ORDER = [z * N_Y + (y + N_Y // 2) % N_Y for z in PLANES for y in range(N_Y)]
-PAIR = 2 * SUB
+def natural_of(p):
+    return (p // N_Y + N_Z // 2) % N_Z * N_Y + (p % N_Y + N_Y // 2) % N_Y
 
 
 def chip_of(p):
     return (p + N_X // 2) % N_X
 
 
+ORDER = [natural_of(p) for p in range(N_FSDP)]
+PAIR = 2 * SUB
+
+
 def hbm():
     return pl.BlockSpec(memory_space=pl.ANY)
 
@@ -31,7 +34,8 @@
     return pl.BlockSpec(memory_space=pltpu.VMEM)
 
 
-def pair_kernel(own, other, pair):
+def pair_kernel(own, other, *refs):
+    pair = refs[-1]
     core = lax.rem(lax.axis_index("rep"), 2)
     for p in range(N_X):
         columns = pl.ds(pl.multiple_of((2 * chip_of(p) + core) * SIDE, SIDE), SIDE)
@@ -39,19 +43,59 @@
         pair[p] = total.astype(jnp.bfloat16)
 
 
-def add_pair(own, other):
+def add_pair(own, other, *after):
     return pl.pallas_call(
         pair_kernel,
         out_shape=jax.ShapeDtypeStruct((N_X, BLOCKS, SUB, SIDE), jnp.bfloat16),
-        in_specs=[vmem(), vmem()],
+        in_specs=[vmem(), vmem()] + [vmem()] * len(after),
         out_specs=vmem(),
         compiler_params=pltpu.CompilerParams(vmem_limit_bytes=16 * 1024 * 1024),
         name="add_pair",
-    )(own, other)
+    )(own, other, *after)
+
+
+def place_kernel(places, pieces, outgoing):
+    outgoing[...] = jnp.zeros_like(outgoing)
+    for b in range(BLOCKS):
+        outgoing[places[b]] = pieces[b]
+
+
+def place_blocks(places, pieces):
+    return pl.pallas_call(
+        place_kernel,
+        out_shape=jax.ShapeDtypeStruct((N_FSDP, SUB, SIDE), jnp.bfloat16),
+        in_specs=[pl.BlockSpec(memory_space=pltpu.SMEM), vmem()],
+        out_specs=vmem(),
+        compiler_params=pltpu.CompilerParams(vmem_limit_bytes=16 * 1024 * 1024),
+        name="place_blocks",
+    )(places, pieces)
+
+
+def pick_kernel(places, returned, update, sems):
+    copies = [
+        pltpu.make_async_copy(returned.at[places[b]], update.at[b], sems.at[b])
+        for b in range(BLOCKS)
+    ]
+    for c in copies:
+        c.start()
+    for c in copies:
+        c.wait()
+
+
+def pick_blocks(places, returned):
+    return pl.pallas_call(
+        pick_kernel,
+        out_shape=jax.ShapeDtypeStruct((BLOCKS, SUB, SIDE), jnp.bfloat16),
+        in_specs=[pl.BlockSpec(memory_space=pltpu.SMEM), vmem()],
+        out_specs=hbm(),
+        scratch_shapes=[pltpu.SemaphoreType.DMA((BLOCKS,))],
+        compiler_params=pltpu.CompilerParams(vmem_limit_bytes=16 * 1024 * 1024),
+        name="pick_blocks",
+    )(places, returned)
 
 
 def step_kernel(
-    arrived, left, left_turned, right, right_turned, first, second,
+    arrived, left, left_turned, right, first, second,
     first_new_hbm, second_new_hbm, leaving,
     grad, first_new, second_new, ratio, sems,
 ):
@@ -79,9 +123,9 @@
     for c in stores:
         c.start()
     back = jnp.dot(left[...], ratio[...], preferred_element_type=jnp.float32).astype(jnp.bfloat16)
-    block_update = jnp.dot(back, right_turned[...], preferred_element_type=jnp.float32).astype(
-        jnp.bfloat16
-    )
+    block_update = lax.dot_general(
+        back, right[...], (((1,), (1,)), ((), ())), preferred_element_type=jnp.float32
+    ).astype(jnp.bfloat16)
     for here, natural in places:
         leaving[here, :] = block_update[natural, :]
     for c in stores:
@@ -93,7 +137,7 @@
     return pl.pallas_call(
         step_kernel,
         out_shape=(square, square, square),
-        in_specs=[vmem()] * 7,
+        in_specs=[vmem()] * 6,
         out_specs=(hbm(), hbm(), vmem()),
         scratch_shapes=[pltpu.VMEM((SIDE, SIDE), jnp.bfloat16)] * 4 + [pltpu.SemaphoreType.DMA((2,))],
         compiler_params=pltpu.CompilerParams(vmem_limit_bytes=24 * 1024 * 1024),
@@ -108,35 +152,36 @@
     return lax.all_to_all(pieces, "fsdp", 0, 0, axis_index_groups=[ORDER], tiled=True)
 
 
+def sum_over_x(pair):
+    chips = [[2 * chip_of(p) + core for p in range(N_X)] for core in range(2)]
+    parts = lax.all_to_all(pair, "rep", 0, 0, axis_index_groups=chips, tiled=True)
+    return jnp.sum(parts.astype(jnp.float32), axis=0).astype(jnp.bfloat16)
+
+
 def local(partials, left_basis, right_basis, first_moment, second_moment, owners):
-    owner_row = lax.dynamic_slice_in_dim(owners, lax.axis_index("rep"), 1, 0)[0]
-    slots = jnp.array(ORDER, jnp.int32)
-    selector = (owner_row[None, :] == slots[:, None]).astype(jnp.bfloat16)
+    n_rep = 2 * N_X
+    rep = lax.axis_index("rep")
+    core = lax.rem(rep, 2)
+    owner_row = lax.dynamic_slice_in_dim(owners, rep, 1, 0)[0]
+    places = natural_of(owner_row)
     left = left_basis[0, 0]
     right = right_basis[0, 0]
 
     own = partials[0]
-    other = lax.ppermute(own, "rep", [(i, i ^ 1) for i in range(2 * N_X)])
-    other, left_turned, right_turned, selector = lax.optimization_barrier(
-        (other, left.T, right.T, selector)
-    )
+    other = lax.ppermute(own, "rep", [(i, i ^ 1) for i in range(n_rep)])
+    other, left_turned, places = lax.optimization_barrier((other, left.T, places))
     pair = add_pair(own, other)
-    chips = [[2 * chip_of(p) + core for p in range(N_X)] for core in range(2)]
-    parts = lax.all_to_all(pair, "rep", 0, 0, axis_index_groups=chips, tiled=True)
-    pieces = jnp.sum(parts.astype(jnp.float32), axis=0).astype(jnp.bfloat16)
-
-    outgoing = jnp.einsum(
-        "qb,bsk->qsk", selector, pieces, preferred_element_type=jnp.float32
-    ).astype(jnp.bfloat16)
-    arrived = exchange(outgoing)
+    early = lax.cond(core == 1, sum_over_x, lambda p: jnp.zeros(p.shape[1:], p.dtype), pair)
+    follow = lax.ppermute(early[0], "rep", [(i + 1, i) for i in range(0, n_rep, 2)])
+    pair = add_pair(own, other, follow)
+    pieces = lax.cond(core == 0, lambda p, e: sum_over_x(p), lambda p, e: e, pair, early)
+
+    arrived = exchange(place_blocks(places, pieces))
     first_new, second_new, leaving = step(
-        arrived.reshape(SIDE, SIDE), left, left_turned, right, right_turned,
-        first_moment[0, 0], second_moment[0, 0],
+        arrived.reshape(SIDE, SIDE), left, left_turned, right, first_moment[0, 0], second_moment[0, 0]
     )
     returned = exchange(leaving.reshape(N_FSDP, SUB, SIDE))
-    update = jnp.einsum(
-        "qb,qsk->bsk", selector, returned, preferred_element_type=jnp.float32
-    ).astype(jnp.bfloat16)
+    update = pick_blocks(places, returned)
     return (first_new[None, None], second_new[None, None], update)
 
 

time: 106 us -> 97.1 us (0.916)
  blocking collectives: 95.9 us -> 70.9 us
  waiting for transfers between devices: 0.01 us -> 15 us
  local copies, waits for them, and re-layouts: 4.1 us -> 1.3 us
  Pallas kernels: 2.37 us -> 4.36 us
  starting transfers between devices: 1.92 us -> 3.34 us
    all_to_all x2, blocking collectives: 79.1 us -> 60.3 us  [exchange(): lax.all_to_all(pieces, 'fsdp', 0, 0, axis_index_groups=[ORDER], tiled=True)]
    ppermute x1 -> x2, waiting for transfers between devices: 0.01 us -> 15 us  [the longest x1 14.2 us: local(): lax.ppermute(early[0], 'rep', [(i + 1, i) for i in range(0, n_rep, 2)])]
    all_to_all x1, blocking collectives: 16.8 us -> 10.6 us  [sum_over_x(): lax.all_to_all(pair, 'rep', 0, 0, axis_index_groups=chips, tiled=True)]
    unnamed x19 -> x11, local copies, waits for them, and re-layouts: 3.8 us -> 1.28 us
    pallas_call x0 -> x2, Pallas kernels: none -> 1.92 us  [the longest x1 1.34 us: pick_blocks(): pl.pallas_call(pick_kernel, out_shape=jax.ShapeDtypeStruct((BLOCKS, SUB,...]
    ppermute x1 -> x2, starting transfers between devices: 1.92 us -> 3.34 us  [the longest x1 2.05 us: local(): other = lax.ppermute(own, 'rep', [(i, i ^ 1) for i in range(n_rep)])]
  transfers between devices with their start and end apart: 1 -> 2, of which waited for: 0 -> 2; matrix products, arithmetic and copies ran while one was open for 2% -> 2% of each run, Pallas kernels for 0% -> 0%
where the time goes in v3:
time: 97.1 us; the launch traced here: 96.5 us
  blocking collectives  70.9 us (73%)
  waiting for transfers between devices  15 us (15%)
  Pallas kernels  4.36 us (4%)
  starting transfers between devices  3.34 us (3%)
  local copies, waits for them, and re-layouts  1.3 us (1%)
    all_to_all x2, blocking collectives, exchange(): lax.all_to_all(pieces, 'fsdp', 0, 0, axis_index_groups=[ORDER], tiled=True)  60.3 us
    ppermute x1, waiting for transfers between devices, local(): lax.ppermute(early[0], 'rep', [(i + 1, i) for i in range(0, n_rep, 2)])  14.2 us
    all_to_all x1, blocking collectives, sum_over_x(): lax.all_to_all(pair, 'rep', 0, 0, axis_index_groups=chips, tiled=True)  10.6 us
    pallas_call x1, Pallas kernels, step(): pl.pallas_call(step_kernel, out_shape=(square, square, square), in_specs=...  2.2 us
    ppermute x1, starting transfers between devices, local(): other = lax.ppermute(own, 'rep', [(i, i ^ 1) for i in range(n_rep)])  2.05 us
  transfers between devices with their start and end apart: 2, of which 2 were waited for; matrix products, arithmetic and copies ran while one was open for 2% of the time, Pallas kernels for 0%

profile of v3, /device:TPU:6, one launch (start us, length us, event | category | flops | bytes accessed | tf_op | source)
XLA Modules:
  0.0 96.5 jit_solution(14409397799124486816)
XLA Ops:
  0.6 0.0 copy-start
  0.6 2.1 %collective-permute-start = (bf16[16,8,4096]{2,1,0:T(8,128)(2,1)}, bf16[16,8,4096]{2,1,0:T(8,128)(2,1)S(1)}, u32[]{:S(2)}, u32[]{:S(2)}) collective-permute-start(bf16[16,8,4096]{2,1,0:T(8,128)(2,1)} %bitcast.27), channel_id=1, source_target_pairs={{0,64},{64,0},{128,192},{192,128},{256,320},{320,256},{384,448},{4... | collective-permute-start | bytes 3145736 | tf_op jit(solution)/shard_map/ppermute | solution.py:171
  2.7 1.3 %copy.9 = bf16[1,1,512,512]{2,3,1,0:T(8,128)(2,1)S(1)} copy(bf16[1,1,512,512]{3,2,1,0:T(8,128)(2,1)} %param.11) | data formatting | bytes 1048576 | tf_op args[1]
  4.0 0.7 fusion.places
  4.7 0.9 collective-permute-done.other
  5.5 0.0 copy-done
  5.5 0.1 add_pair.2
  5.7 1.3 %collective-permute-start.1 = (bf16[8,512]{1,0:T(8,128)(2,1)S(1)}, bf16[8,512]{1,0:T(8,128)(2,1)S(1)}, u32[]{:S(2)}, u32[]{:S(2)}) collective-permute-start(bf16[8,512]{1,0:T(8,128)(2,1)S(1)} %slice_bitcast_fusion), channel_id=1, source_target_pairs={{64,0},{192,128},{320,256},{448,384},{65,1},{193,129},{321,257},{4... | collective-permute-start | bytes 24584 | tf_op jit(solution)/shard_map/ppermute | solution.py:175
  7.0 14.2 %collective-permute-done.1.refs_0_ = bf16[8,512]{1,0:T(8,128)(2,1)S(1)} collective-permute-done((bf16[8,512]{1,0:T(8,128)(2,1)S(1)}, bf16[8,512]{1,0:T(8,128)(2,1)S(1)}, u32[]{:S(2)}, u32[]{:S(2)}) %collective-permute-start.1) | collective-permute-done | bytes 8224 | tf_op jit(solution)/shard_map/ppermute | solution.py:175
  21.2 0.1 add_pair.3
  21.3 0.0 copy-start.4
  21.3 10.7 %conditional.3 = (bf16[16,8,512]{2,1,0:T(8,128)(2,1)S(1)}) conditional(s32[]{:T(128)} %convert_element_type.6, bf16[16,8,512]{2,1,0:T(8,128)(2,1)S(1)} %get-tuple-element.24, bf16[4,16,8,512]{3,2,1,0:T(8,128)(2,1)S(1)} %add_pair.3), branch_computations={%region_3.4_spmd, %region_4.6_spmd} | conditional | flops 196608 | bytes 1703946 | solution.py:177
  21.3 10.6 %all_to_all.19 = bf16[4,16,8,512]{3,2,1,0:T(8,128)(2,1)S(1)} all-to-all(bf16[4,16,8,512]{3,2,1,0:T(8,128)(2,1)S(1)} %param.3), channel_id=1, replica_groups={{256,384,0,128},{320,448,64,192},{257,385,1,129},{321,449,65,193},{258,..., dimensions={0} | all-to-all | bytes 1048576 | tf_op jit(solution)/shard_map/cond/branch_1_fun/all_to_all | solution.py:157
  32.0 0.1 reduce_sum.23
  32.0 0.0 copy-start.3
  32.0 0.6 place_blocks.1
  32.6 0.0 copy-start.1
  32.6 0.0 copy-start.2
  32.7 31.7 %all_to_all.20 = bf16[64,8,512]{2,1,0:T(8,128)(2,1)S(1)} all-to-all(bf16[64,8,512]{2,1,0:T(8,128)(2,1)S(1)} %place_blocks.1), channel_id=1, replica_groups={{34,35,32,33,38,39,36,37,42,43,40,41,46,47,44,45,50,51,48,49,54,55,52,5..., dimensions={0} | all-to-all | bytes 1048576 | tf_op jit(solution)/shard_map/all_to_all | solution.py:152
  64.3 0.0 copy-done.4
  64.3 0.0 copy-done.1
  64.4 2.2 %soap_step.1 = (bf16[512,512]{1,0:T(8,128)(2,1)}, bf16[512,512]{1,0:T(8,128)(2,1)}, bf16[512,512]{1,0:T(8,128)(2,1)S(1)}) custom-call(bf16[512,512]{1,0:T(8,128)(2,1)S(1)} %bitcast.32, bf16[512,512]{1,0:T(8,128)(2,1)S(1)} %bitcast.30, bf16[512,512]{1,0:T(8,128)(2,1)S(1)} %bitcast.31, bf16[512,512]{1,0:T(8,128)(2,1)S(1)} %bitcast.34, ...), custom_call_target="tpu_custom_call" | custom-call | flops 1073741824 | bytes 4718592 | tf_op jit(solution)/shard_map/soap_step/pallas_call | solution.py:137
  66.6 28.6 %all_to_all.21.returned = bf16[64,8,512]{2,1,0:T(8,128)(2,1)S(1)} all-to-all(bf16[64,8,512]{2,1,0:T(8,128)(2,1)S(1)} %bitcast.33), channel_id=1, replica_groups={{34,35,32,33,38,39,36,37,42,43,40,41,46,47,44,45,50,51,48,49,54,55,52,5..., dimensions={0} | all-to-all | bytes 1048576 | tf_op jit(solution)/shard_map/all_to_all | solution.py:152
  95.2 1.3 %pick_blocks.1 = bf16[16,8,512]{2,1,0:T(8,128)(2,1)} custom-call(s32[16]{0:T(128)S(1)} %fusion.places, bf16[64,8,512]{2,1,0:T(8,128)(2,1)S(1)} %all_to_all.21.returned), custom_call_target="tpu_custom_call" | custom-call | tf_op jit(solution)/shard_map/pick_blocks/pallas_call | solution.py:86
  (5 shorter events, 0.1 us)
Async XLA Ops:
  0.6 4.9 %copy-start = (bf16[1,16,8,4096]{3,2,1,0:T(8,128)(2,1)S(1)}, bf16[1,16,8,4096]{3,2,1,0:T(8,128)(2,1)}, u32[]{:S(2)}) copy-start(bf16[1,16,8,4096]{3,2,1,0:T(8,128)(2,1)} %param.10) | copy-start | bytes 3145732
  0.6 4.9 %collective-permute-start = (bf16[16,8,4096]{2,1,0:T(8,128)(2,1)}, bf16[16,8,4096]{2,1,0:T(8,128)(2,1)S(1)}, u32[]{:S(2)}, u32[]{:S(2)}) collective-permute-start(bf16[16,8,4096]{2,1,0:T(8,128)(2,1)} %bitcast.27), channel_id=1, source_target_pairs={{0,64},{64,0},{128,192},{192,128},{256,320},{320,256},{384,448},{4... | collective-permute-start | bytes 3145736 | tf_op jit(solution)/shard_map/ppermute | solution.py:171
  5.7 15.5 %collective-permute-start.1 = (bf16[8,512]{1,0:T(8,128)(2,1)S(1)}, bf16[8,512]{1,0:T(8,128)(2,1)S(1)}, u32[]{:S(2)}, u32[]{:S(2)}) collective-permute-start(bf16[8,512]{1,0:T(8,128)(2,1)S(1)} %slice_bitcast_fusion), channel_id=1, source_target_pairs={{64,0},{192,128},{320,256},{448,384},{65,1},{193,129},{321,257},{4... | collective-permute-start | bytes 24584 | tf_op jit(solution)/shard_map/ppermute | solution.py:175
  21.3 43.0 %copy-start.4 = (bf16[1,1,512,512]{3,2,1,0:T(8,128)(2,1)S(1)}, bf16[1,1,512,512]{3,2,1,0:T(8,128)(2,1)}, u32[]{:S(2)}) copy-start(bf16[1,1,512,512]{3,2,1,0:T(8,128)(2,1)} %param.14) | copy-start | bytes 1572868
  32.0 32.3 %copy-start.3 = (bf16[1,1,512,512]{3,2,1,0:T(8,128)(2,1)S(1)}, bf16[1,1,512,512]{3,2,1,0:T(8,128)(2,1)}, u32[]{:S(2)}) copy-start(bf16[1,1,512,512]{3,2,1,0:T(8,128)(2,1)} %param.13) | copy-start | bytes 1572868
  32.6 31.7 %copy-start.1 = (bf16[1,1,512,512]{3,2,1,0:T(8,128)(2,1)S(1)}, bf16[1,1,512,512]{3,2,1,0:T(8,128)(2,1)}, u32[]{:S(2)}) copy-start(bf16[1,1,512,512]{3,2,1,0:T(8,128)(2,1)} %param.11) | copy-start | bytes 1572868
  32.6 31.7 %copy-start.2 = (bf16[1,1,512,512]{3,2,1,0:T(8,128)(2,1)S(1)}, bf16[1,1,512,512]{3,2,1,0:T(8,128)(2,1)}, u32[]{:S(2)}) copy-start(bf16[1,1,512,512]{3,2,1,0:T(8,128)(2,1)} %param.12) | copy-start | bytes 1572868

commit v4 on v3

--- a/solution.py
+++ b/solution.py
@@ -55,7 +55,6 @@
 
 
 def place_kernel(places, pieces, outgoing):
-    outgoing[...] = jnp.zeros_like(outgoing)
     for b in range(BLOCKS):
         outgoing[places[b]] = pieces[b]
 
@@ -71,31 +70,8 @@
     )(places, pieces)
 
 
-def pick_kernel(places, returned, update, sems):
-    copies = [
-        pltpu.make_async_copy(returned.at[places[b]], update.at[b], sems.at[b])
-        for b in range(BLOCKS)
-    ]
-    for c in copies:
-        c.start()
-    for c in copies:
-        c.wait()
-
-
-def pick_blocks(places, returned):
-    return pl.pallas_call(
-        pick_kernel,
-        out_shape=jax.ShapeDtypeStruct((BLOCKS, SUB, SIDE), jnp.bfloat16),
-        in_specs=[pl.BlockSpec(memory_space=pltpu.SMEM), vmem()],
-        out_specs=hbm(),
-        scratch_shapes=[pltpu.SemaphoreType.DMA((BLOCKS,))],
-        compiler_params=pltpu.CompilerParams(vmem_limit_bytes=16 * 1024 * 1024),
-        name="pick_blocks",
-    )(places, returned)
-
-
 def step_kernel(
-    arrived, left, left_turned, right, first, second,
+    owned, arrived, left, left_turned, right, first, second,
     first_new_hbm, second_new_hbm, leaving,
     grad, first_new, second_new, ratio, sems,
 ):
@@ -111,11 +87,12 @@
     for i in range(SIDE // STRIP):
         rows = slice(i * STRIP, (i + 1) * STRIP)
         rotated = jnp.dot(turned[rows], right[...], preferred_element_type=jnp.float32)
+        rotated = jnp.where(owned[0] == 1, rotated, 0.0)
         one = 0.95 * first[rows, :].astype(jnp.float32) + 0.05 * rotated
         two = 0.95 * second[rows, :].astype(jnp.float32) + 0.05 * rotated * rotated
         first_new[rows, :] = one.astype(jnp.bfloat16)
         second_new[rows, :] = two.astype(jnp.bfloat16)
-        ratio[rows, :] = (one / (jnp.sqrt(two) + 1e-08)).astype(jnp.bfloat16)
+        ratio[rows, :] = (one / (two * lax.rsqrt(two) + 1e-08)).astype(jnp.bfloat16)
     stores = [
         pltpu.make_async_copy(first_new, first_new_hbm, sems.at[0]),
         pltpu.make_async_copy(second_new, second_new_hbm, sems.at[1]),
@@ -137,7 +114,7 @@
     return pl.pallas_call(
         step_kernel,
         out_shape=(square, square, square),
-        in_specs=[vmem()] * 6,
+        in_specs=[pl.BlockSpec(memory_space=pltpu.SMEM)] + [vmem()] * 6,
         out_specs=(hbm(), hbm(), vmem()),
         scratch_shapes=[pltpu.VMEM((SIDE, SIDE), jnp.bfloat16)] * 4 + [pltpu.SemaphoreType.DMA((2,))],
         compiler_params=pltpu.CompilerParams(vmem_limit_bytes=24 * 1024 * 1024),
@@ -164,12 +141,17 @@
     core = lax.rem(rep, 2)
     owner_row = lax.dynamic_slice_in_dim(owners, rep, 1, 0)[0]
     places = natural_of(owner_row)
+    slots = jnp.arange(N_FSDP, dtype=jnp.int32)
+    selector = (places[None, :] == slots[:, None]).astype(jnp.bfloat16)
+    owned = jnp.any(owner_row == lax.axis_index("fsdp")).astype(jnp.int32).reshape(1)
     left = left_basis[0, 0]
     right = right_basis[0, 0]
 
     own = partials[0]
     other = lax.ppermute(own, "rep", [(i, i ^ 1) for i in range(n_rep)])
-    other, left_turned, places = lax.optimization_barrier((other, left.T, places))
+    other, left_turned, places, selector, owned = lax.optimization_barrier(
+        (other, left.T, places, selector, owned)
+    )
     pair = add_pair(own, other)
     early = lax.cond(core == 1, sum_over_x, lambda p: jnp.zeros(p.shape[1:], p.dtype), pair)
     follow = lax.ppermute(early[0], "rep", [(i + 1, i) for i in range(0, n_rep, 2)])
@@ -178,10 +160,13 @@
 
     arrived = exchange(place_blocks(places, pieces))
     first_new, second_new, leaving = step(
-        arrived.reshape(SIDE, SIDE), left, left_turned, right, first_moment[0, 0], second_moment[0, 0]
+        owned, arrived.reshape(SIDE, SIDE), left, left_turned, right,
+        first_moment[0, 0], second_moment[0, 0],
     )
     returned = exchange(leaving.reshape(N_FSDP, SUB, SIDE))
-    update = pick_blocks(places, returned)
+    update = jnp.einsum(
+        "qb,qsk->bsk", selector, returned, preferred_element_type=jnp.float32
+    ).astype(jnp.bfloat16)
     return (first_new[None, None], second_new[None, None], update)
 
 

time: 97.1 us -> 99 us (1.020)
  other arithmetic: 0.8 us -> 2.92 us
  Pallas kernels: 4.36 us -> 2.88 us
    pallas_call x1 -> x0, Pallas kernels: 1.34 us -> none  [pick_blocks(): pl.pallas_call(pick_kernel, out_shape=jax.ShapeDtypeStruct((BLOCKS, SUB,...]
    reduce_or x0 -> x1, other arithmetic: none -> 1.33 us  [local(): jnp.any(owner_row == lax.axis_index('fsdp')).astype(jnp.int32).reshape(1)]
    unnamed x11 -> x12, local copies, waits for them, and re-layouts: 1.28 us -> 2.02 us
  transfers between devices with their start and end apart: 2 -> 2, of which waited for: 2 -> 1; matrix products, arithmetic and copies ran while one was open for 2% -> 4% of each run, Pallas kernels for 0% -> 0%
where the time goes in v4:
time: 99 us; the launch traced here: 98.3 us
  blocking collectives  70.9 us (72%)
  waiting for transfers between devices  14.5 us (15%)
  starting transfers between devices  3.34 us (3%)
  other arithmetic  2.92 us (3%)
  Pallas kernels  2.88 us (3%)
  local copies, waits for them, and re-layouts  2.03 us (2%)
  between operations  1.42 us (1%)
    all_to_all x2, blocking collectives, exchange(): lax.all_to_all(pieces, 'fsdp', 0, 0, axis_index_groups=[ORDER], tiled=True)  60.3 us
    ppermute x1, waiting for transfers between devices, local(): lax.ppermute(early[0], 'rep', [(i + 1, i) for i in range(0, n_rep, 2)])  14.5 us
    all_to_all x1, blocking collectives, sum_over_x(): lax.all_to_all(pair, 'rep', 0, 0, axis_index_groups=chips, tiled=True)  10.6 us
    pallas_call x1, Pallas kernels, step(): pl.pallas_call(step_kernel, out_shape=(square, square, square), in_specs=...  2.07 us
    ppermute x1, starting transfers between devices, local(): other = lax.ppermute(own, 'rep', [(i, i ^ 1) for i in range(n_rep)])  2.05 us
    unnamed x12, local copies, waits for them, and re-layouts  2.02 us
  transfers between devices with their start and end apart: 2, of which 1 were waited for; matrix products, arithmetic and copies ran while one was open for 4% of the time, Pallas kernels for 0%

profile of v4, /device:TPU:6, one launch (start us, length us, event | category | flops | bytes accessed | tf_op | source)
XLA Modules:
  0.0 98.3 jit_solution(5976409670065744228)
XLA Ops:
  0.6 2.1 %collective-permute-start = (bf16[16,8,4096]{2,1,0:T(8,128)(2,1)}, bf16[16,8,4096]{2,1,0:T(8,128)(2,1)S(1)}, u32[]{:S(2)}, u32[]{:S(2)}) collective-permute-start(bf16[16,8,4096]{2,1,0:T(8,128)(2,1)} %bitcast.34), channel_id=1, source_target_pairs={{0,64},{64,0},{128,192},{192,128},{256,320},{320,256},{384,448},{4... | collective-permute-start | bytes 3145736 | tf_op jit(solution)/shard_map/ppermute | solution.py:151
  2.7 1.3 %compare_reduce_fusion = pred[]{:T(512)} fusion(s32[]{:T(128)S(6)} %axis_index.25, s32[8,16]{1,0:T(8,128)} %param.15, s32[]{:T(128)S(6)} %select_n.35), kind=kLoop, calls=%fused_computation.14 | loop fusion | flops 31 | bytes 73 | tf_op jit(solution)/shard_map/reduce_or | solution.py:146
  4.7 1.3 %copy.13 = bf16[1,1,512,512]{2,3,1,0:T(8,128)(2,1)S(1)} copy(bf16[1,1,512,512]{3,2,1,0:T(8,128)(2,1)} %param.11) | data formatting | bytes 1048576 | tf_op args[1]
  5.9 0.7 fusion.3.places
  6.7 0.7 fusion.13
  7.4 0.1 fusion.1
  7.5 0.0 collective-permute-done.other
  7.5 0.1 add_pair.2
  7.7 1.3 %collective-permute-start.1 = (bf16[8,512]{1,0:T(8,128)(2,1)S(1)}, bf16[8,512]{1,0:T(8,128)(2,1)S(1)}, u32[]{:S(2)}, u32[]{:S(2)}) collective-permute-start(bf16[8,512]{1,0:T(8,128)(2,1)S(1)} %slice_bitcast_fusion), channel_id=1, source_target_pairs={{64,0},{192,128},{320,256},{448,384},{65,1},{193,129},{321,257},{4... | collective-permute-start | bytes 24584 | tf_op jit(solution)/shard_map/ppermute | solution.py:157
  9.0 14.5 %collective-permute-done.1.refs_0_ = bf16[8,512]{1,0:T(8,128)(2,1)S(1)} collective-permute-done((bf16[8,512]{1,0:T(8,128)(2,1)S(1)}, bf16[8,512]{1,0:T(8,128)(2,1)S(1)}, u32[]{:S(2)}, u32[]{:S(2)}) %collective-permute-start.1) | collective-permute-done | bytes 8224 | tf_op jit(solution)/shard_map/ppermute | solution.py:157
  23.5 0.1 add_pair.3
  23.6 0.0 copy-start.4
  23.6 10.7 %conditional.3 = (bf16[16,8,512]{2,1,0:T(8,128)(2,1)S(1)}) conditional(s32[]{:T(128)} %convert_element_type.18, bf16[16,8,512]{2,1,0:T(8,128)(2,1)S(1)} %get-tuple-element.34, bf16[4,16,8,512]{3,2,1,0:T(8,128)(2,1)S(1)} %add_pair.3), branch_computations={%region_4.5_spmd, %region_5.7_spmd} | conditional | flops 196608 | bytes 1703946 | solution.py:159
  23.6 10.6 %all_to_all.19 = bf16[4,16,8,512]{3,2,1,0:T(8,128)(2,1)S(1)} all-to-all(bf16[4,16,8,512]{3,2,1,0:T(8,128)(2,1)S(1)} %param.3), channel_id=1, replica_groups={{256,384,0,128},{320,448,64,192},{257,385,1,129},{321,449,65,193},{258,..., dimensions={0} | all-to-all | bytes 1048576 | tf_op jit(solution)/shard_map/cond/branch_1_fun/all_to_all | solution.py:134
  34.3 0.1 reduce_sum.23
  34.3 0.0 copy-start.3
  34.4 0.6 place_blocks.1
  34.9 0.0 copy-start.1
  34.9 0.0 copy-start.2
  34.9 31.7 %all_to_all.20 = bf16[64,8,512]{2,1,0:T(8,128)(2,1)S(1)} all-to-all(bf16[64,8,512]{2,1,0:T(8,128)(2,1)S(1)} %place_blocks.1), channel_id=1, replica_groups={{34,35,32,33,38,39,36,37,42,43,40,41,46,47,44,45,50,51,48,49,54,55,52,5..., dimensions={0} | all-to-all | bytes 1048576 | tf_op jit(solution)/shard_map/all_to_all | solution.py:129
  66.6 2.1 %soap_step.1 = (bf16[512,512]{1,0:T(8,128)(2,1)}, bf16[512,512]{1,0:T(8,128)(2,1)}, bf16[512,512]{1,0:T(8,128)(2,1)S(1)}) custom-call(s32[1]{0:T(128)} %bitcast.5.owned, bf16[512,512]{1,0:T(8,128)(2,1)S(1)} %bitcast.39, bf16[512,512]{1,0:T(8,128)(2,1)S(1)} %bitcast.37, bf16[512,512]{1,0:T(8,128)(2,1)S(1)} %bitcast.38, bf16[512,512]{1,0:T(8,128)(2,1)S(1)} %bitcast.41, ...), custom_call_target="tpu_custom_call" | custom-call | flops 1073741824 | bytes 4718592 | tf_op jit(solution)/shard_map/soap_step/pallas_call | solution.py:114
  68.7 28.6 %all_to_all.21 = bf16[64,8,512]{2,1,0:T(8,128)(2,1)S(1)} all-to-all(bf16[64,8,512]{2,1,0:T(8,128)(2,1)S(1)} %bitcast.40), channel_id=1, replica_groups={{34,35,32,33,38,39,36,37,42,43,40,41,46,47,44,45,50,51,48,49,54,55,52,5..., dimensions={0} | all-to-all | bytes 1048576 | tf_op jit(solution)/shard_map/all_to_all | solution.py:129
  97.3 0.3 convolution_convert_fusion
  97.6 0.7 copy.16
  (9 shorter events, 0.1 us)
Async XLA Ops:
  0.6 6.8 %copy-start = (bf16[1,16,8,4096]{3,2,1,0:T(8,128)(2,1)S(1)}, bf16[1,16,8,4096]{3,2,1,0:T(8,128)(2,1)}, u32[]{:S(2)}) copy-start(bf16[1,16,8,4096]{3,2,1,0:T(8,128)(2,1)} %param.10) | copy-start | bytes 3145732
  0.6 6.8 %collective-permute-start = (bf16[16,8,4096]{2,1,0:T(8,128)(2,1)}, bf16[16,8,4096]{2,1,0:T(8,128)(2,1)S(1)}, u32[]{:S(2)}, u32[]{:S(2)}) collective-permute-start(bf16[16,8,4096]{2,1,0:T(8,128)(2,1)} %bitcast.34), channel_id=1, source_target_pairs={{0,64},{64,0},{128,192},{192,128},{256,320},{320,256},{384,448},{4... | collective-permute-start | bytes 3145736 | tf_op jit(solution)/shard_map/ppermute | solution.py:151
  7.7 15.8 %collective-permute-start.1 = (bf16[8,512]{1,0:T(8,128)(2,1)S(1)}, bf16[8,512]{1,0:T(8,128)(2,1)S(1)}, u32[]{:S(2)}, u32[]{:S(2)}) collective-permute-start(bf16[8,512]{1,0:T(8,128)(2,1)S(1)} %slice_bitcast_fusion), channel_id=1, source_target_pairs={{64,0},{192,128},{320,256},{448,384},{65,1},{193,129},{321,257},{4... | collective-permute-start | bytes 24584 | tf_op jit(solution)/shard_map/ppermute | solution.py:157
  23.6 43.0 %copy-start.4 = (bf16[1,1,512,512]{3,2,1,0:T(8,128)(2,1)S(1)}, bf16[1,1,512,512]{3,2,1,0:T(8,128)(2,1)}, u32[]{:S(2)}) copy-start(bf16[1,1,512,512]{3,2,1,0:T(8,128)(2,1)} %param.14) | copy-start | bytes 1572868
  34.3 32.3 %copy-start.3 = (bf16[1,1,512,512]{3,2,1,0:T(8,128)(2,1)S(1)}, bf16[1,1,512,512]{3,2,1,0:T(8,128)(2,1)}, u32[]{:S(2)}) copy-start(bf16[1,1,512,512]{3,2,1,0:T(8,128)(2,1)} %param.13) | copy-start | bytes 1572868
  34.9 31.7 %copy-start.1 = (bf16[1,1,512,512]{3,2,1,0:T(8,128)(2,1)S(1)}, bf16[1,1,512,512]{3,2,1,0:T(8,128)(2,1)}, u32[]{:S(2)}) copy-start(bf16[1,1,512,512]{3,2,1,0:T(8,128)(2,1)} %param.11) | copy-start | bytes 1572868
  34.9 31.7 %copy-start.2 = (bf16[1,1,512,512]{3,2,1,0:T(8,128)(2,1)S(1)}, bf16[1,1,512,512]{3,2,1,0:T(8,128)(2,1)}, u32[]{:S(2)}) copy-start(bf16[1,1,512,512]{3,2,1,0:T(8,128)(2,1)} %param.12) | copy-start | bytes 1572868

commit v5 on v4

--- a/solution.py
+++ b/solution.py
@@ -54,12 +54,14 @@
     )(own, other, *after)
 
 
-def place_kernel(places, pieces, outgoing):
+def place_kernel(owners, pieces, outgoing):
+    rep = lax.axis_index("rep")
+    outgoing[...] = jnp.zeros_like(outgoing)
     for b in range(BLOCKS):
-        outgoing[places[b]] = pieces[b]
+        outgoing[natural_of(owners[rep, b])] = pieces[b]
 
 
-def place_blocks(places, pieces):
+def place_blocks(owners, pieces):
     return pl.pallas_call(
         place_kernel,
         out_shape=jax.ShapeDtypeStruct((N_FSDP, SUB, SIDE), jnp.bfloat16),
@@ -67,11 +69,11 @@
         out_specs=vmem(),
         compiler_params=pltpu.CompilerParams(vmem_limit_bytes=16 * 1024 * 1024),
         name="place_blocks",
-    )(places, pieces)
+    )(owners, pieces)
 
 
 def step_kernel(
-    owned, arrived, left, left_turned, right, first, second,
+    arrived, left, left_turned, right, first, second,
     first_new_hbm, second_new_hbm, leaving,
     grad, first_new, second_new, ratio, sems,
 ):
@@ -87,7 +89,6 @@
     for i in range(SIDE // STRIP):
         rows = slice(i * STRIP, (i + 1) * STRIP)
         rotated = jnp.dot(turned[rows], right[...], preferred_element_type=jnp.float32)
-        rotated = jnp.where(owned[0] == 1, rotated, 0.0)
         one = 0.95 * first[rows, :].astype(jnp.float32) + 0.05 * rotated
         two = 0.95 * second[rows, :].astype(jnp.float32) + 0.05 * rotated * rotated
         first_new[rows, :] = one.astype(jnp.bfloat16)
@@ -114,7 +115,7 @@
     return pl.pallas_call(
         step_kernel,
         out_shape=(square, square, square),
-        in_specs=[pl.BlockSpec(memory_space=pltpu.SMEM)] + [vmem()] * 6,
+        in_specs=[vmem()] * 6,
         out_specs=(hbm(), hbm(), vmem()),
         scratch_shapes=[pltpu.VMEM((SIDE, SIDE), jnp.bfloat16)] * 4 + [pltpu.SemaphoreType.DMA((2,))],
         compiler_params=pltpu.CompilerParams(vmem_limit_bytes=24 * 1024 * 1024),
@@ -140,27 +141,23 @@
     rep = lax.axis_index("rep")
     core = lax.rem(rep, 2)
     owner_row = lax.dynamic_slice_in_dim(owners, rep, 1, 0)[0]
-    places = natural_of(owner_row)
-    slots = jnp.arange(N_FSDP, dtype=jnp.int32)
-    selector = (places[None, :] == slots[:, None]).astype(jnp.bfloat16)
-    owned = jnp.any(owner_row == lax.axis_index("fsdp")).astype(jnp.int32).reshape(1)
+    slots = natural_of(jnp.arange(N_FSDP, dtype=jnp.int32))
+    selector = (owner_row[None, :] == slots[:, None]).astype(jnp.bfloat16)
     left = left_basis[0, 0]
     right = right_basis[0, 0]
 
     own = partials[0]
     other = lax.ppermute(own, "rep", [(i, i ^ 1) for i in range(n_rep)])
-    other, left_turned, places, selector, owned = lax.optimization_barrier(
-        (other, left.T, places, selector, owned)
-    )
+    other, left_turned, selector = lax.optimization_barrier((other, left.T, selector))
     pair = add_pair(own, other)
     early = lax.cond(core == 1, sum_over_x, lambda p: jnp.zeros(p.shape[1:], p.dtype), pair)
     follow = lax.ppermute(early[0], "rep", [(i + 1, i) for i in range(0, n_rep, 2)])
     pair = add_pair(own, other, follow)
     pieces = lax.cond(core == 0, lambda p, e: sum_over_x(p), lambda p, e: e, pair, early)
 
-    arrived = exchange(place_blocks(places, pieces))
+    arrived = exchange(place_blocks(owners, pieces))
     first_new, second_new, leaving = step(
-        owned, arrived.reshape(SIDE, SIDE), left, left_turned, right,
+        arrived.reshape(SIDE, SIDE), left, left_turned, right,
         first_moment[0, 0], second_moment[0, 0],
     )
     returned = exchange(leaving.reshape(N_FSDP, SUB, SIDE))

time: 99 us -> 96.8 us (0.978)
  other arithmetic: 2.92 us -> 0.16 us
  waiting for transfers between devices: 14.5 us -> 15.6 us
    ppermute x1, waiting for transfers between devices: 0.01 us -> 1.44 us  [local(): other = lax.ppermute(own, 'rep', [(i, i ^ 1) for i in range(n_rep)])]
    reduce_or x1 -> x0, other arithmetic: 1.33 us -> none  [local(): jnp.any(owner_row == lax.axis_index('fsdp')).astype(jnp.int32).reshape(1)]
    unnamed x12 -> x14, local copies, waits for them, and re-layouts: 2.02 us -> 2.03 us
  transfers between devices with their start and end apart: 2 -> 2, of which waited for: 1 -> 2; matrix products, arithmetic and copies ran while one was open for 4% -> 1% of each run, Pallas kernels for 0% -> 0%
where the time goes in v5:
time: 96.8 us; the launch traced here: 96.2 us
  blocking collectives  70.9 us (73%)
  waiting for transfers between devices  15.6 us (16%)
  starting transfers between devices  3.34 us (3%)
  Pallas kernels  3.06 us (3%)
  local copies, waits for them, and re-layouts  2.05 us (2%)
    all_to_all x2, blocking collectives, exchange(): lax.all_to_all(pieces, 'fsdp', 0, 0, axis_index_groups=[ORDER], tiled=True)  60.3 us
    ppermute x1, waiting for transfers between devices, local(): lax.ppermute(early[0], 'rep', [(i + 1, i) for i in range(0, n_rep, 2)])  14.2 us
    all_to_all x1, blocking collectives, sum_over_x(): lax.all_to_all(pair, 'rep', 0, 0, axis_index_groups=chips, tiled=True)  10.6 us
    ppermute x1, starting transfers between devices, local(): other = lax.ppermute(own, 'rep', [(i, i ^ 1) for i in range(n_rep)])  2.05 us
    unnamed x14, local copies, waits for them, and re-layouts  2.03 us
    pallas_call x1, Pallas kernels, step(): pl.pallas_call(step_kernel, out_shape=(square, square, square), in_specs=...  2.01 us
  transfers between devices with their start and end apart: 2, of which 2 were waited for; matrix products, arithmetic and copies ran while one was open for 1% of the time, Pallas kernels for 0%

profile of v5, /device:TPU:6, one launch (start us, length us, event | category | flops | bytes accessed | tf_op | source)
XLA Modules:
  0.0 96.2 jit_solution(16869481795437150322)
XLA Ops:
  0.6 0.0 copy-start
  0.6 2.1 %collective-permute-start = (bf16[16,8,4096]{2,1,0:T(8,128)(2,1)}, bf16[16,8,4096]{2,1,0:T(8,128)(2,1)S(1)}, u32[]{:S(2)}, u32[]{:S(2)}) collective-permute-start(bf16[16,8,4096]{2,1,0:T(8,128)(2,1)} %bitcast.19), channel_id=1, source_target_pairs={{0,64},{64,0},{128,192},{192,128},{256,320},{320,256},{384,448},{4... | collective-permute-start | bytes 3145736 | tf_op jit(solution)/shard_map/ppermute | solution.py:150
  2.7 0.0 copy-start.2
  2.7 1.3 %copy.13 = bf16[1,1,512,512]{2,3,1,0:T(8,128)(2,1)S(1)} copy(bf16[1,1,512,512]{3,2,1,0:T(8,128)(2,1)} %param.11) | data formatting | bytes 1048576 | tf_op args[1]
  4.0 0.1 compare_convert_fusion
  4.1 1.4 %collective-permute-done.other = bf16[16,8,4096]{2,1,0:T(8,128)(2,1)S(1)} collective-permute-done((bf16[16,8,4096]{2,1,0:T(8,128)(2,1)}, bf16[16,8,4096]{2,1,0:T(8,128)(2,1)S(1)}, u32[]{:S(2)}, u32[]{:S(2)}) %collective-permute-start) | collective-permute-done | bytes 1048608 | tf_op jit(solution)/shard_map/ppermute | solution.py:150
  5.5 0.1 add_pair.2
  5.7 1.3 %collective-permute-start.1 = (bf16[8,512]{1,0:T(8,128)(2,1)S(1)}, bf16[8,512]{1,0:T(8,128)(2,1)S(1)}, u32[]{:S(2)}, u32[]{:S(2)}) collective-permute-start(bf16[8,512]{1,0:T(8,128)(2,1)S(1)} %slice_bitcast_fusion), channel_id=1, source_target_pairs={{64,0},{192,128},{320,256},{448,384},{65,1},{193,129},{321,257},{4... | collective-permute-start | bytes 24584 | tf_op jit(solution)/shard_map/ppermute | solution.py:154
  7.0 14.2 %collective-permute-done.1.refs_0_ = bf16[8,512]{1,0:T(8,128)(2,1)S(1)} collective-permute-done((bf16[8,512]{1,0:T(8,128)(2,1)S(1)}, bf16[8,512]{1,0:T(8,128)(2,1)S(1)}, u32[]{:S(2)}, u32[]{:S(2)}) %collective-permute-start.1) | collective-permute-done | bytes 8224 | tf_op jit(solution)/shard_map/ppermute | solution.py:154
  21.2 0.1 add_pair.3
  21.3 0.0 copy-start.5
  21.3 10.7 %conditional.3 = (bf16[16,8,512]{2,1,0:T(8,128)(2,1)S(1)}) conditional(s32[]{:T(128)} %convert_element_type.16, bf16[16,8,512]{2,1,0:T(8,128)(2,1)S(1)} %get-tuple-element.30, bf16[4,16,8,512]{3,2,1,0:T(8,128)(2,1)S(1)} %add_pair.3), branch_computations={%region_3.4_spmd, %region_4.6_spmd} | conditional | flops 196608 | bytes 1703946 | solution.py:156
  21.3 10.6 %all_to_all.19 = bf16[4,16,8,512]{3,2,1,0:T(8,128)(2,1)S(1)} all-to-all(bf16[4,16,8,512]{3,2,1,0:T(8,128)(2,1)S(1)} %param.3), channel_id=1, replica_groups={{256,384,0,128},{320,448,64,192},{257,385,1,129},{321,449,65,193},{258,..., dimensions={0} | all-to-all | bytes 1048576 | tf_op jit(solution)/shard_map/cond/branch_1_fun/all_to_all | solution.py:135
  32.0 0.1 reduce_sum.23
  32.0 0.0 copy-start.4
  32.0 0.8 place_blocks.1
  32.9 0.0 copy-start.1
  32.9 0.0 copy-start.3
  32.9 31.7 %all_to_all.20 = bf16[64,8,512]{2,1,0:T(8,128)(2,1)S(1)} all-to-all(bf16[64,8,512]{2,1,0:T(8,128)(2,1)S(1)} %place_blocks.1), channel_id=1, replica_groups={{34,35,32,33,38,39,36,37,42,43,40,41,46,47,44,45,50,51,48,49,54,55,52,5..., dimensions={0} | all-to-all | bytes 1048576 | tf_op jit(solution)/shard_map/all_to_all | solution.py:130
  64.6 0.0 copy-done.3
  64.6 2.0 %soap_step.1 = (bf16[512,512]{1,0:T(8,128)(2,1)}, bf16[512,512]{1,0:T(8,128)(2,1)}, bf16[512,512]{1,0:T(8,128)(2,1)S(1)}) custom-call(bf16[512,512]{1,0:T(8,128)(2,1)S(1)} %bitcast.24, bf16[512,512]{1,0:T(8,128)(2,1)S(1)} %bitcast.22, bf16[512,512]{1,0:T(8,128)(2,1)S(1)} %bitcast.23, bf16[512,512]{1,0:T(8,128)(2,1)S(1)} %bitcast.26, ...), custom_call_target="tpu_custom_call" | custom-call | flops 1073741824 | bytes 4718592 | tf_op jit(solution)/shard_map/soap_step/pallas_call | solution.py:115
  66.6 28.6 %all_to_all.21 = bf16[64,8,512]{2,1,0:T(8,128)(2,1)S(1)} all-to-all(bf16[64,8,512]{2,1,0:T(8,128)(2,1)S(1)} %bitcast.25), channel_id=1, replica_groups={{34,35,32,33,38,39,36,37,42,43,40,41,46,47,44,45,50,51,48,49,54,55,52,5..., dimensions={0} | all-to-all | bytes 1048576 | tf_op jit(solution)/shard_map/all_to_all | solution.py:130
  95.2 0.3 convolution_convert_fusion
  95.5 0.7 copy.16
  (10 shorter events, 0.1 us)
Async XLA Ops:
  0.6 4.9 %copy-start = (bf16[1,16,8,4096]{3,2,1,0:T(8,128)(2,1)S(1)}, bf16[1,16,8,4096]{3,2,1,0:T(8,128)(2,1)}, u32[]{:S(2)}) copy-start(bf16[1,16,8,4096]{3,2,1,0:T(8,128)(2,1)} %param.10) | copy-start | bytes 3145732
  0.6 4.9 %collective-permute-start = (bf16[16,8,4096]{2,1,0:T(8,128)(2,1)}, bf16[16,8,4096]{2,1,0:T(8,128)(2,1)S(1)}, u32[]{:S(2)}, u32[]{:S(2)}) collective-permute-start(bf16[16,8,4096]{2,1,0:T(8,128)(2,1)} %bitcast.19), channel_id=1, source_target_pairs={{0,64},{64,0},{128,192},{192,128},{256,320},{320,256},{384,448},{4... | collective-permute-start | bytes 3145736 | tf_op jit(solution)/shard_map/ppermute | solution.py:150
  2.7 1.3 %copy-start.2 = (s32[8,16]{1,0:T(8,128)S(1)}, s32[8,16]{1,0:T(8,128)}, u32[]{:S(2)}) copy-start(s32[8,16]{1,0:T(8,128)} %owners.1) | copy-start | bytes 1540
  5.7 15.5 %collective-permute-start.1 = (bf16[8,512]{1,0:T(8,128)(2,1)S(1)}, bf16[8,512]{1,0:T(8,128)(2,1)S(1)}, u32[]{:S(2)}, u32[]{:S(2)}) collective-permute-start(bf16[8,512]{1,0:T(8,128)(2,1)S(1)} %slice_bitcast_fusion), channel_id=1, source_target_pairs={{64,0},{192,128},{320,256},{448,384},{65,1},{193,129},{321,257},{4... | collective-permute-start | bytes 24584 | tf_op jit(solution)/shard_map/ppermute | solution.py:154
  21.3 43.3 %copy-start.5 = (bf16[1,1,512,512]{3,2,1,0:T(8,128)(2,1)S(1)}, bf16[1,1,512,512]{3,2,1,0:T(8,128)(2,1)}, u32[]{:S(2)}) copy-start(bf16[1,1,512,512]{3,2,1,0:T(8,128)(2,1)} %param.14) | copy-start | bytes 1572868
  32.0 32.5 %copy-start.4 = (bf16[1,1,512,512]{3,2,1,0:T(8,128)(2,1)S(1)}, bf16[1,1,512,512]{3,2,1,0:T(8,128)(2,1)}, u32[]{:S(2)}) copy-start(bf16[1,1,512,512]{3,2,1,0:T(8,128)(2,1)} %param.13) | copy-start | bytes 1572868
  32.9 31.7 %copy-start.1 = (bf16[1,1,512,512]{3,2,1,0:T(8,128)(2,1)S(1)}, bf16[1,1,512,512]{3,2,1,0:T(8,128)(2,1)}, u32[]{:S(2)}) copy-start(bf16[1,1,512,512]{3,2,1,0:T(8,128)(2,1)} %param.11) | copy-start | bytes 1572868
  32.9 31.7 %copy-start.3 = (bf16[1,1,512,512]{3,2,1,0:T(8,128)(2,1)S(1)}, bf16[1,1,512,512]{3,2,1,0:T(8,128)(2,1)}, u32[]{:S(2)}) copy-start(bf16[1,1,512,512]{3,2,1,0:T(8,128)(2,1)} %param.12) | copy-start | bytes 1572868

commit v6 on v5

--- a/solution.py
+++ b/solution.py
@@ -14,16 +14,13 @@
 BLOCKS = 16
 STRIP = 128
 
-def natural_of(p):
-    return (p // N_Y + N_Z // 2) % N_Z * N_Y + (p % N_Y + N_Y // 2) % N_Y
+PLANES = [8, 0, 1, 15, 2, 14, 3, 13, 4, 12, 5, 11, 6, 10, 7, 9]
+ORDER = [z * N_Y + (y + N_Y // 2) % N_Y for z in PLANES for y in range(N_Y)]
+PAIR = 2 * SUB
 
 
 def chip_of(p):
     return (p + N_X // 2) % N_X
-
-
-ORDER = [natural_of(p) for p in range(N_FSDP)]
-PAIR = 2 * SUB
 
 
 def hbm():
@@ -52,24 +49,6 @@
         compiler_params=pltpu.CompilerParams(vmem_limit_bytes=16 * 1024 * 1024),
         name="add_pair",
     )(own, other, *after)
-
-
-def place_kernel(owners, pieces, outgoing):
-    rep = lax.axis_index("rep")
-    outgoing[...] = jnp.zeros_like(outgoing)
-    for b in range(BLOCKS):
-        outgoing[natural_of(owners[rep, b])] = pieces[b]
-
-
-def place_blocks(owners, pieces):
-    return pl.pallas_call(
-        place_kernel,
-        out_shape=jax.ShapeDtypeStruct((N_FSDP, SUB, SIDE), jnp.bfloat16),
-        in_specs=[pl.BlockSpec(memory_space=pltpu.SMEM), vmem()],
-        out_specs=vmem(),
-        compiler_params=pltpu.CompilerParams(vmem_limit_bytes=16 * 1024 * 1024),
-        name="place_blocks",
-    )(owners, pieces)
 
 
 def step_kernel(
@@ -141,7 +120,7 @@
     rep = lax.axis_index("rep")
     core = lax.rem(rep, 2)
     owner_row = lax.dynamic_slice_in_dim(owners, rep, 1, 0)[0]
-    slots = natural_of(jnp.arange(N_FSDP, dtype=jnp.int32))
+    slots = jnp.array(ORDER, jnp.int32)
     selector = (owner_row[None, :] == slots[:, None]).astype(jnp.bfloat16)
     left = left_basis[0, 0]
     right = right_basis[0, 0]
@@ -155,7 +134,10 @@
     pair = add_pair(own, other, follow)
     pieces = lax.cond(core == 0, lambda p, e: sum_over_x(p), lambda p, e: e, pair, early)
 
-    arrived = exchange(place_blocks(owners, pieces))
+    outgoing = jnp.einsum(
+        "qb,bsk->qsk", selector, pieces, preferred_element_type=jnp.float32
+    ).astype(jnp.bfloat16)
+    arrived = exchange(outgoing)
     first_new, second_new, leaving = step(
         arrived.reshape(SIDE, SIDE), left, left_turned, right,
         first_moment[0, 0], second_moment[0, 0],

time: 96.8 us -> 96.5 us (level)
  local copies, waits for them, and re-layouts: 2.05 us -> 3.02 us
    unnamed x14 -> x16, local copies, waits for them, and re-layouts: 2.03 us -> 2.66 us
where the time goes in v6:
time: 96.5 us; the launch traced here: 95.9 us
  blocking collectives  70.6 us (73%)
  waiting for transfers between devices  15 us (16%)
  starting transfers between devices  3.34 us (3%)
  local copies, waits for them, and re-layouts  3.02 us (3%)
  Pallas kernels  2.31 us (2%)
    all_to_all x2, blocking collectives, exchange(): lax.all_to_all(pieces, 'fsdp', 0, 0, axis_index_groups=[ORDER], tiled=True)  60.1 us
    ppermute x1, waiting for transfers between devices, local(): lax.ppermute(early[0], 'rep', [(i + 1, i) for i in range(0, n_rep, 2)])  14.2 us
    all_to_all x1, blocking collectives, sum_over_x(): lax.all_to_all(pair, 'rep', 0, 0, axis_index_groups=chips, tiled=True)  10.5 us
    unnamed x16, local copies, waits for them, and re-layouts  2.66 us
    pallas_call x1, Pallas kernels, step(): pl.pallas_call(step_kernel, out_shape=(square, square, square), in_specs=...  2.06 us
    ppermute x1, starting transfers between devices, local(): other = lax.ppermute(own, 'rep', [(i, i ^ 1) for i in range(n_rep)])  2.05 us
  transfers between devices with their start and end apart: 2, of which 2 were waited for; matrix products, arithmetic and copies ran while one was open for 1% of the time, Pallas kernels for 0%

profile of v6, /device:TPU:6, one launch (start us, length us, event | category | flops | bytes accessed | tf_op | source)
XLA Modules:
  0.0 95.9 jit_solution(8605996890144952526)
XLA Ops:
  0.6 0.0 copy-start
  0.7 2.1 %collective-permute-start = (bf16[16,8,4096]{2,1,0:T(8,128)(2,1)}, bf16[16,8,4096]{2,1,0:T(8,128)(2,1)S(1)}, u32[]{:S(2)}, u32[]{:S(2)}) collective-permute-start(bf16[16,8,4096]{2,1,0:T(8,128)(2,1)} %bitcast.22), channel_id=1, source_target_pairs={{0,64},{64,0},{128,192},{192,128},{256,320},{320,256},{384,448},{4... | collective-permute-start | bytes 3145736 | tf_op jit(solution)/shard_map/ppermute | solution.py:129
  2.7 1.3 %copy.16 = bf16[1,1,512,512]{2,3,1,0:T(8,128)(2,1)S(1)} copy(bf16[1,1,512,512]{3,2,1,0:T(8,128)(2,1)} %param.12) | data formatting | bytes 1048576 | tf_op args[1]
  4.0 0.0 copy-start.6
  4.0 0.6 copy-done.6
  4.6 0.1 compare_convert_fusion
  4.7 0.8 collective-permute-done.other
  5.6 0.1 add_pair.2
  5.7 1.3 %collective-permute-start.1 = (bf16[8,512]{1,0:T(8,128)(2,1)S(1)}, bf16[8,512]{1,0:T(8,128)(2,1)S(1)}, u32[]{:S(2)}, u32[]{:S(2)}) collective-permute-start(bf16[8,512]{1,0:T(8,128)(2,1)S(1)} %slice_bitcast_fusion), channel_id=1, source_target_pairs={{64,0},{192,128},{320,256},{448,384},{65,1},{193,129},{321,257},{4... | collective-permute-start | bytes 24584 | tf_op jit(solution)/shard_map/ppermute | solution.py:133
  7.0 14.2 %collective-permute-done.1.refs_0_ = bf16[8,512]{1,0:T(8,128)(2,1)S(1)} collective-permute-done((bf16[8,512]{1,0:T(8,128)(2,1)S(1)}, bf16[8,512]{1,0:T(8,128)(2,1)S(1)}, u32[]{:S(2)}, u32[]{:S(2)}) %collective-permute-start.1) | collective-permute-done | bytes 8224 | tf_op jit(solution)/shard_map/ppermute | solution.py:133
  21.2 0.1 add_pair.3
  21.3 10.6 %conditional.3 = (bf16[16,8,512]{2,0,1:T(8,128)(2,1)S(1)}) conditional(s32[]{:T(128)} %convert_element_type.20, bf16[16,8,512]{2,1,0:T(8,128)(2,1)S(1)} %get-tuple-element.33, bf16[4,16,8,512]{3,2,1,0:T(8,128)(2,1)S(1)} %add_pair.3), branch_computations={%region_3.0_spmd, %region_4.0_spmd} | conditional | flops 196608 | bytes 1966090 | solution.py:135
  21.3 10.5 %all_to_all.19 = bf16[4,16,8,512]{3,2,1,0:T(8,128)(2,1)S(1)} all-to-all(bf16[4,16,8,512]{3,2,1,0:T(8,128)(2,1)S(1)} %param.3), channel_id=1, replica_groups={{256,384,0,128},{320,448,64,192},{257,385,1,129},{321,449,65,193},{258,..., dimensions={0} | all-to-all | bytes 1048576 | tf_op jit(solution)/shard_map/cond/branch_1_fun/all_to_all | solution.py:114
  31.8 0.1 reduce_sum.23
  32.0 0.3 convolution_convert_fusion
  32.3 0.0 copy-start.5
  32.3 0.3 copy.18
  32.6 0.0 copy-start.2
  32.6 0.0 copy-start.3
  32.6 31.6 %all_to_all.20 = bf16[64,8,512]{2,1,0:T(8,128)(2,1)S(1)} all-to-all(bf16[64,8,512]{2,1,0:T(8,128)(2,1)S(1)} %copy.18), channel_id=1, replica_groups={{34,35,32,33,2,3,0,1,6,7,4,5,62,63,60,61,10,11,8,9,58,59,56,57,14,15,12..., dimensions={0} | all-to-all | bytes 1048576 | tf_op jit(solution)/shard_map/all_to_all | solution.py:109
  64.2 2.1 %soap_step.1 = (bf16[512,512]{1,0:T(8,128)(2,1)}, bf16[512,512]{1,0:T(8,128)(2,1)}, bf16[512,512]{1,0:T(8,128)(2,1)S(1)}) custom-call(bf16[512,512]{1,0:T(8,128)(2,1)S(1)} %bitcast.27, bf16[512,512]{1,0:T(8,128)(2,1)S(1)} %bitcast.25, bf16[512,512]{1,0:T(8,128)(2,1)S(1)} %bitcast.26, bf16[512,512]{1,0:T(8,128)(2,1)S(1)} %bitcast.29, ...), custom_call_target="tpu_custom_call" | custom-call | flops 1073741824 | bytes 4718592 | tf_op jit(solution)/shard_map/soap_step/pallas_call | solution.py:94
  66.3 28.6 %all_to_all.21 = bf16[64,8,512]{2,1,0:T(8,128)(2,1)S(1)} all-to-all(bf16[64,8,512]{2,1,0:T(8,128)(2,1)S(1)} %bitcast.28), channel_id=1, replica_groups={{34,35,32,33,2,3,0,1,6,7,4,5,62,63,60,61,10,11,8,9,58,59,56,57,14,15,12..., dimensions={0} | all-to-all | bytes 1048576 | tf_op jit(solution)/shard_map/all_to_all | solution.py:109
  94.9 0.3 convolution_convert_fusion.1
  95.2 0.7 copy.21
  (13 shorter events, 0.1 us)
Async XLA Ops:
  0.6 3.4 %copy-start = (s32[8,16]{1,0:T(8,128)S(1)}, s32[8,16]{1,0:T(8,128)}, u32[]{:S(2)}) copy-start(s32[8,16]{1,0:T(8,128)} %param.16) | copy-start | bytes 1540
  0.6 4.9 %copy-start.1 = (bf16[1,16,8,4096]{3,2,1,0:T(8,128)(2,1)S(1)}, bf16[1,16,8,4096]{3,2,1,0:T(8,128)(2,1)}, u32[]{:S(2)}) copy-start(bf16[1,16,8,4096]{3,2,1,0:T(8,128)(2,1)} %param.11) | copy-start | bytes 3145732
  0.7 4.9 %collective-permute-start = (bf16[16,8,4096]{2,1,0:T(8,128)(2,1)}, bf16[16,8,4096]{2,1,0:T(8,128)(2,1)S(1)}, u32[]{:S(2)}, u32[]{:S(2)}) collective-permute-start(bf16[16,8,4096]{2,1,0:T(8,128)(2,1)} %bitcast.22), channel_id=1, source_target_pairs={{0,64},{64,0},{128,192},{192,128},{256,320},{320,256},{384,448},{4... | collective-permute-start | bytes 3145736 | tf_op jit(solution)/shard_map/ppermute | solution.py:129
  4.0 0.7 copy-start.6
  5.7 15.5 %collective-permute-start.1 = (bf16[8,512]{1,0:T(8,128)(2,1)S(1)}, bf16[8,512]{1,0:T(8,128)(2,1)S(1)}, u32[]{:S(2)}, u32[]{:S(2)}) collective-permute-start(bf16[8,512]{1,0:T(8,128)(2,1)S(1)} %slice_bitcast_fusion), channel_id=1, source_target_pairs={{64,0},{192,128},{320,256},{448,384},{65,1},{193,129},{321,257},{4... | collective-permute-start | bytes 24584 | tf_op jit(solution)/shard_map/ppermute | solution.py:133
  32.3 31.9 %copy-start.4 = (bf16[1,1,512,512]{3,2,1,0:T(8,128)(2,1)S(1)}, bf16[1,1,512,512]{3,2,1,0:T(8,128)(2,1)}, u32[]{:S(2)}) copy-start(bf16[1,1,512,512]{3,2,1,0:T(8,128)(2,1)} %param.14) | copy-start | bytes 1572868
  32.3 31.9 %copy-start.5 = (bf16[1,1,512,512]{3,2,1,0:T(8,128)(2,1)S(1)}, bf16[1,1,512,512]{3,2,1,0:T(8,128)(2,1)}, u32[]{:S(2)}) copy-start(bf16[1,1,512,512]{3,2,1,0:T(8,128)(2,1)} %param.15) | copy-start | bytes 1572868
  32.6 31.6 %copy-start.2 = (bf16[1,1,512,512]{3,2,1,0:T(8,128)(2,1)S(1)}, bf16[1,1,512,512]{3,2,1,0:T(8,128)(2,1)}, u32[]{:S(2)}) copy-start(bf16[1,1,512,512]{3,2,1,0:T(8,128)(2,1)} %param.12) | copy-start | bytes 1572868
  32.6 31.6 %copy-start.3 = (bf16[1,1,512,512]{3,2,1,0:T(8,128)(2,1)S(1)}, bf16[1,1,512,512]{3,2,1,0:T(8,128)(2,1)}, u32[]{:S(2)}) copy-start(bf16[1,1,512,512]{3,2,1,0:T(8,128)(2,1)} %param.13) | copy-start | bytes 1572868

commit v7 on v6

--- a/solution.py
+++ b/solution.py
@@ -12,15 +12,18 @@
 SUB = 8
 SIDE = 512
 BLOCKS = 16
-STRIP = 128
+STRIP = 256
 
-PLANES = [8, 0, 1, 15, 2, 14, 3, 13, 4, 12, 5, 11, 6, 10, 7, 9]
-ORDER = [z * N_Y + (y + N_Y // 2) % N_Y for z in PLANES for y in range(N_Y)]
-PAIR = 2 * SUB
+def natural_of(p):
+    return (p // N_Y + N_Z // 2) % N_Z * N_Y + (p % N_Y + N_Y // 2) % N_Y
 
 
 def chip_of(p):
     return (p + N_X // 2) % N_X
+
+
+ORDER = [natural_of(p) for p in range(N_FSDP)]
+PAIR = 2 * SUB
 
 
 def hbm():
@@ -54,7 +57,7 @@
 def step_kernel(
     arrived, left, left_turned, right, first, second,
     first_new_hbm, second_new_hbm, leaving,
-    grad, first_new, second_new, ratio, sems,
+    grad, first_new, second_new, sems,
 ):
     places = [
         (slice(p * SUB, p * SUB + PAIR), slice(ORDER[p] * SUB, ORDER[p] * SUB + PAIR))
@@ -62,24 +65,27 @@
     ]
     for here, natural in places:
         grad[natural, :] = arrived[here, :]
-    turned = jnp.dot(left_turned[...], grad[...], preferred_element_type=jnp.float32).astype(
-        jnp.bfloat16
-    )
-    for i in range(SIDE // STRIP):
-        rows = slice(i * STRIP, (i + 1) * STRIP)
-        rotated = jnp.dot(turned[rows], right[...], preferred_element_type=jnp.float32)
+    strips = [slice(i, i + STRIP) for i in range(0, SIDE, STRIP)]
+    total = None
+    for rows in strips:
+        turned = jnp.dot(
+            left_turned[rows, :], grad[...], preferred_element_type=jnp.float32
+        ).astype(jnp.bfloat16)
+        rotated = jnp.dot(turned, right[...], preferred_element_type=jnp.float32)
         one = 0.95 * first[rows, :].astype(jnp.float32) + 0.05 * rotated
         two = 0.95 * second[rows, :].astype(jnp.float32) + 0.05 * rotated * rotated
         first_new[rows, :] = one.astype(jnp.bfloat16)
         second_new[rows, :] = two.astype(jnp.bfloat16)
-        ratio[rows, :] = (one / (two * lax.rsqrt(two) + 1e-08)).astype(jnp.bfloat16)
+        ratio = (one / (two * lax.rsqrt(two) + 1e-08)).astype(jnp.bfloat16)
+        part = jnp.dot(left[:, rows], ratio, preferred_element_type=jnp.float32)
+        total = part if total is None else total + part
     stores = [
         pltpu.make_async_copy(first_new, first_new_hbm, sems.at[0]),
         pltpu.make_async_copy(second_new, second_new_hbm, sems.at[1]),
     ]
     for c in stores:
         c.start()
-    back = jnp.dot(left[...], ratio[...], preferred_element_type=jnp.float32).astype(jnp.bfloat16)
+    back = total.astype(jnp.bfloat16)
     block_update = lax.dot_general(
         back, right[...], (((1,), (1,)), ((), ())), preferred_element_type=jnp.float32
     ).astype(jnp.bfloat16)
@@ -96,7 +102,7 @@
         out_shape=(square, square, square),
         in_specs=[vmem()] * 6,
         out_specs=(hbm(), hbm(), vmem()),
-        scratch_shapes=[pltpu.VMEM((SIDE, SIDE), jnp.bfloat16)] * 4 + [pltpu.SemaphoreType.DMA((2,))],
+        scratch_shapes=[pltpu.VMEM((SIDE, SIDE), jnp.bfloat16)] * 3 + [pltpu.SemaphoreType.DMA((2,))],
         compiler_params=pltpu.CompilerParams(vmem_limit_bytes=24 * 1024 * 1024),
         cost_estimate=pl.CostEstimate(
             flops=8 * SIDE**3, bytes_accessed=18 * SIDE**2, transcendentals=2 * SIDE**2
@@ -120,7 +126,7 @@
     rep = lax.axis_index("rep")
     core = lax.rem(rep, 2)
     owner_row = lax.dynamic_slice_in_dim(owners, rep, 1, 0)[0]
-    slots = jnp.array(ORDER, jnp.int32)
+    slots = natural_of(jnp.arange(N_FSDP, dtype=jnp.int32))
     selector = (owner_row[None, :] == slots[:, None]).astype(jnp.bfloat16)
     left = left_basis[0, 0]
     right = right_basis[0, 0]

time: 96.5 us -> 96.6 us (level)
    unnamed x16 -> x14, local copies, waits for them, and re-layouts: 2.66 us -> 2.03 us
where the time goes in v7:
time: 96.6 us; the launch traced here: 96 us
  blocking collectives  70.7 us (73%)
  waiting for transfers between devices  15.6 us (16%)
  starting transfers between devices  3.34 us (3%)
  local copies, waits for them, and re-layouts  2.39 us (2%)
  Pallas kernels  2.36 us (2%)
    all_to_all x2, blocking collectives, exchange(): lax.all_to_all(pieces, 'fsdp', 0, 0, axis_index_groups=[ORDER], tiled=True)  60.2 us
    ppermute x1, waiting for transfers between devices, local(): lax.ppermute(early[0], 'rep', [(i + 1, i) for i in range(0, n_rep, 2)])  14.2 us
    all_to_all x1, blocking collectives, sum_over_x(): lax.all_to_all(pair, 'rep', 0, 0, axis_index_groups=chips, tiled=True)  10.5 us
    pallas_call x1, Pallas kernels, step(): pl.pallas_call(step_kernel, out_shape=(square, square, square), in_specs=...  2.12 us
    ppermute x1, starting transfers between devices, local(): other = lax.ppermute(own, 'rep', [(i, i ^ 1) for i in range(n_rep)])  2.05 us
    unnamed x14, local copies, waits for them, and re-layouts  2.03 us
  transfers between devices with their start and end apart: 2, of which 2 were waited for; matrix products, arithmetic and copies ran while one was open for 1% of the time, Pallas kernels for 0%

profile of v7, /device:TPU:6, one launch (start us, length us, event | category | flops | bytes accessed | tf_op | source)
XLA Modules:
  0.0 96.0 jit_solution(2496123479580267590)
XLA Ops:
  0.6 0.0 copy-start
  0.7 2.1 %collective-permute-start = (bf16[16,8,4096]{2,1,0:T(8,128)(2,1)}, bf16[16,8,4096]{2,1,0:T(8,128)(2,1)S(1)}, u32[]{:S(2)}, u32[]{:S(2)}) collective-permute-start(bf16[16,8,4096]{2,1,0:T(8,128)(2,1)} %bitcast.22), channel_id=1, source_target_pairs={{0,64},{64,0},{128,192},{192,128},{256,320},{320,256},{384,448},{4... | collective-permute-start | bytes 3145736 | tf_op jit(solution)/shard_map/ppermute | solution.py:135
  2.7 1.3 %copy.15 = bf16[1,1,512,512]{2,3,1,0:T(8,128)(2,1)S(1)} copy(bf16[1,1,512,512]{3,2,1,0:T(8,128)(2,1)} %param.11) | data formatting | bytes 1048576 | tf_op args[1]
  4.0 0.1 compare_convert_fusion
  4.1 1.5 %collective-permute-done.other = bf16[16,8,4096]{2,1,0:T(8,128)(2,1)S(1)} collective-permute-done((bf16[16,8,4096]{2,1,0:T(8,128)(2,1)}, bf16[16,8,4096]{2,1,0:T(8,128)(2,1)S(1)}, u32[]{:S(2)}, u32[]{:S(2)}) %collective-permute-start) | collective-permute-done | bytes 1048608 | tf_op jit(solution)/shard_map/ppermute | solution.py:135
  5.6 0.0 copy-done.1
  5.6 0.1 add_pair.2
  5.7 1.3 %collective-permute-start.1 = (bf16[8,512]{1,0:T(8,128)(2,1)S(1)}, bf16[8,512]{1,0:T(8,128)(2,1)S(1)}, u32[]{:S(2)}, u32[]{:S(2)}) collective-permute-start(bf16[8,512]{1,0:T(8,128)(2,1)S(1)} %slice_bitcast_fusion), channel_id=1, source_target_pairs={{64,0},{192,128},{320,256},{448,384},{65,1},{193,129},{321,257},{4... | collective-permute-start | bytes 24584 | tf_op jit(solution)/shard_map/ppermute | solution.py:139
  7.0 14.2 %collective-permute-done.1.refs_0_ = bf16[8,512]{1,0:T(8,128)(2,1)S(1)} collective-permute-done((bf16[8,512]{1,0:T(8,128)(2,1)S(1)}, bf16[8,512]{1,0:T(8,128)(2,1)S(1)}, u32[]{:S(2)}, u32[]{:S(2)}) %collective-permute-start.1) | collective-permute-done | bytes 8224 | tf_op jit(solution)/shard_map/ppermute | solution.py:139
  21.2 0.1 add_pair.3
  21.3 10.6 %conditional.3 = (bf16[16,8,512]{2,0,1:T(8,128)(2,1)S(1)}) conditional(s32[]{:T(128)} %convert_element_type.20, bf16[16,8,512]{2,1,0:T(8,128)(2,1)S(1)} %get-tuple-element.33, bf16[4,16,8,512]{3,2,1,0:T(8,128)(2,1)S(1)} %add_pair.3), branch_computations={%region_3.4_spmd, %region_4.6_spmd} | conditional | flops 196608 | bytes 1966090 | solution.py:141
  21.3 10.5 %all_to_all.19 = bf16[4,16,8,512]{3,2,1,0:T(8,128)(2,1)S(1)} all-to-all(bf16[4,16,8,512]{3,2,1,0:T(8,128)(2,1)S(1)} %param.3), channel_id=1, replica_groups={{256,384,0,128},{320,448,64,192},{257,385,1,129},{321,449,65,193},{258,..., dimensions={0} | all-to-all | bytes 1048576 | tf_op jit(solution)/shard_map/cond/branch_1_fun/all_to_all | solution.py:120
  31.8 0.1 reduce_sum.23
  32.0 0.3 convolution_convert_fusion
  32.3 0.0 copy-start.4
  32.3 0.0 copy-start.5
  32.3 0.3 copy.17
  32.6 0.0 copy-start.2
  32.6 0.0 copy-start.3
  32.6 31.7 %all_to_all.20 = bf16[64,8,512]{2,1,0:T(8,128)(2,1)S(1)} all-to-all(bf16[64,8,512]{2,1,0:T(8,128)(2,1)S(1)} %copy.17), channel_id=1, replica_groups={{34,35,32,33,38,39,36,37,42,43,40,41,46,47,44,45,50,51,48,49,54,55,52,5..., dimensions={0} | all-to-all | bytes 1048576 | tf_op jit(solution)/shard_map/all_to_all | solution.py:115
  64.3 2.1 %soap_step.1 = (bf16[512,512]{1,0:T(8,128)(2,1)}, bf16[512,512]{1,0:T(8,128)(2,1)}, bf16[512,512]{1,0:T(8,128)(2,1)S(1)}) custom-call(bf16[512,512]{1,0:T(8,128)(2,1)S(1)} %bitcast.27, bf16[512,512]{1,0:T(8,128)(2,1)S(1)} %bitcast.25, bf16[512,512]{1,0:T(8,128)(2,1)S(1)} %bitcast.26, bf16[512,512]{1,0:T(8,128)(2,1)S(1)} %bitcast.29, ...), custom_call_target="tpu_custom_call" | custom-call | flops 1073741824 | bytes 4718592 | tf_op jit(solution)/shard_map/soap_step/pallas_call | solution.py:100
  66.5 28.5 %all_to_all.21 = bf16[64,8,512]{2,1,0:T(8,128)(2,1)S(1)} all-to-all(bf16[64,8,512]{2,1,0:T(8,128)(2,1)S(1)} %bitcast.28), channel_id=1, replica_groups={{34,35,32,33,38,39,36,37,42,43,40,41,46,47,44,45,50,51,48,49,54,55,52,5..., dimensions={0} | all-to-all | bytes 1048576 | tf_op jit(solution)/shard_map/all_to_all | solution.py:115
  95.0 0.3 convolution_convert_fusion.1
  95.3 0.7 copy.20
  (12 shorter events, 0.1 us)
Async XLA Ops:
  0.6 3.4 %copy-start = (s32[8,16]{1,0:T(8,128)S(1)}, s32[8,16]{1,0:T(8,128)}, u32[]{:S(2)}) copy-start(s32[8,16]{1,0:T(8,128)} %param.15) | copy-start | bytes 1540
  0.6 4.9 %copy-start.1 = (bf16[1,16,8,4096]{3,2,1,0:T(8,128)(2,1)S(1)}, bf16[1,16,8,4096]{3,2,1,0:T(8,128)(2,1)}, u32[]{:S(2)}) copy-start(bf16[1,16,8,4096]{3,2,1,0:T(8,128)(2,1)} %param.10) | copy-start | bytes 3145732
  0.7 4.9 %collective-permute-start = (bf16[16,8,4096]{2,1,0:T(8,128)(2,1)}, bf16[16,8,4096]{2,1,0:T(8,128)(2,1)S(1)}, u32[]{:S(2)}, u32[]{:S(2)}) collective-permute-start(bf16[16,8,4096]{2,1,0:T(8,128)(2,1)} %bitcast.22), channel_id=1, source_target_pairs={{0,64},{64,0},{128,192},{192,128},{256,320},{320,256},{384,448},{4... | collective-permute-start | bytes 3145736 | tf_op jit(solution)/shard_map/ppermute | solution.py:135
  5.7 15.5 %collective-permute-start.1 = (bf16[8,512]{1,0:T(8,128)(2,1)S(1)}, bf16[8,512]{1,0:T(8,128)(2,1)S(1)}, u32[]{:S(2)}, u32[]{:S(2)}) collective-permute-start(bf16[8,512]{1,0:T(8,128)(2,1)S(1)} %slice_bitcast_fusion), channel_id=1, source_target_pairs={{64,0},{192,128},{320,256},{448,384},{65,1},{193,129},{321,257},{4... | collective-permute-start | bytes 24584 | tf_op jit(solution)/shard_map/ppermute | solution.py:139
  32.3 32.0 %copy-start.4 = (bf16[1,1,512,512]{3,2,1,0:T(8,128)(2,1)S(1)}, bf16[1,1,512,512]{3,2,1,0:T(8,128)(2,1)}, u32[]{:S(2)}) copy-start(bf16[1,1,512,512]{3,2,1,0:T(8,128)(2,1)} %param.13) | copy-start | bytes 1572868
  32.3 32.0 %copy-start.5 = (bf16[1,1,512,512]{3,2,1,0:T(8,128)(2,1)S(1)}, bf16[1,1,512,512]{3,2,1,0:T(8,128)(2,1)}, u32[]{:S(2)}) copy-start(bf16[1,1,512,512]{3,2,1,0:T(8,128)(2,1)} %param.14) | copy-start | bytes 1572868
  32.6 31.7 %copy-start.2 = (bf16[1,1,512,512]{3,2,1,0:T(8,128)(2,1)S(1)}, bf16[1,1,512,512]{3,2,1,0:T(8,128)(2,1)}, u32[]{:S(2)}) copy-start(bf16[1,1,512,512]{3,2,1,0:T(8,128)(2,1)} %param.11) | copy-start | bytes 1572868
  32.6 31.7 %copy-start.3 = (bf16[1,1,512,512]{3,2,1,0:T(8,128)(2,1)S(1)}, bf16[1,1,512,512]{3,2,1,0:T(8,128)(2,1)}, u32[]{:S(2)}) copy-start(bf16[1,1,512,512]{3,2,1,0:T(8,128)(2,1)} %param.12) | copy-start | bytes 1572868

commit v8 on v7

--- a/solution.py
+++ b/solution.py
@@ -121,6 +121,13 @@
     return jnp.sum(parts.astype(jnp.float32), axis=0).astype(jnp.bfloat16)
 
 
+def to_owners(pieces, selector):
+    outgoing = jnp.einsum(
+        "qb,bsk->qsk", selector, pieces, preferred_element_type=jnp.float32
+    ).astype(jnp.bfloat16)
+    return exchange(outgoing)
+
+
 def local(partials, left_basis, right_basis, first_moment, second_moment, owners):
     n_rep = 2 * N_X
     rep = lax.axis_index("rep")
@@ -137,13 +144,13 @@
     pair = add_pair(own, other)
     early = lax.cond(core == 1, sum_over_x, lambda p: jnp.zeros(p.shape[1:], p.dtype), pair)
     follow = lax.ppermute(early[0], "rep", [(i + 1, i) for i in range(0, n_rep, 2)])
+    arrived = lax.cond(
+        core == 1, to_owners, lambda e, s: jnp.zeros((N_FSDP, SUB, SIDE), e.dtype), early, selector
+    )
     pair = add_pair(own, other, follow)
-    pieces = lax.cond(core == 0, lambda p, e: sum_over_x(p), lambda p, e: e, pair, early)
-
-    outgoing = jnp.einsum(
-        "qb,bsk->qsk", selector, pieces, preferred_element_type=jnp.float32
-    ).astype(jnp.bfloat16)
-    arrived = exchange(outgoing)
+    arrived = lax.cond(
+        core == 0, lambda p, s, a: to_owners(sum_over_x(p), s), lambda p, s, a: a, pair, selector, arrived
+    )
     first_new, second_new, leaving = step(
         arrived.reshape(SIDE, SIDE), left, left_turned, right,
         first_moment[0, 0], second_moment[0, 0],

time: 96.6 us -> 96.5 us (level)
  no operation moved by 1% of the time
where the time goes in v8:
time: 96.5 us; the launch traced here: 95.9 us
  blocking collectives  70.7 us (73%)
  waiting for transfers between devices  15.5 us (16%)
  starting transfers between devices  3.34 us (3%)
  local copies, waits for them, and re-layouts  2.38 us (2%)
  Pallas kernels  2.36 us (2%)
    all_to_all x2, blocking collectives, exchange(): lax.all_to_all(pieces, 'fsdp', 0, 0, axis_index_groups=[ORDER], tiled=True)  60 us
    ppermute x1, waiting for transfers between devices, local(): lax.ppermute(early[0], 'rep', [(i + 1, i) for i in range(0, n_rep, 2)])  14.1 us
    all_to_all x1, blocking collectives, sum_over_x(): lax.all_to_all(pair, 'rep', 0, 0, axis_index_groups=chips, tiled=True)  10.6 us
    pallas_call x1, Pallas kernels, step(): pl.pallas_call(step_kernel, out_shape=(square, square, square), in_specs=...  2.12 us
    ppermute x1, starting transfers between devices, local(): other = lax.ppermute(own, 'rep', [(i, i ^ 1) for i in range(n_rep)])  2.05 us
    unnamed x14, local copies, waits for them, and re-layouts  2.03 us
  transfers between devices with their start and end apart: 2, of which 2 were waited for; matrix products, arithmetic and copies ran while one was open for 1% of the time, Pallas kernels for 0%

profile of v8, /device:TPU:6, one launch (start us, length us, event | category | flops | bytes accessed | tf_op | source)
XLA Modules:
  0.0 95.9 jit_solution(5012485131171780839)
XLA Ops:
  0.6 0.0 copy-start
  0.7 2.1 %collective-permute-start = (bf16[16,8,4096]{2,1,0:T(8,128)(2,1)}, bf16[16,8,4096]{2,1,0:T(8,128)(2,1)S(1)}, u32[]{:S(2)}, u32[]{:S(2)}) collective-permute-start(bf16[16,8,4096]{2,1,0:T(8,128)(2,1)} %bitcast.28), channel_id=1, source_target_pairs={{0,64},{64,0},{128,192},{192,128},{256,320},{320,256},{384,448},{4... | collective-permute-start | bytes 3145736 | tf_op jit(solution)/shard_map/ppermute | solution.py:142
  2.7 1.3 %copy.25 = bf16[1,1,512,512]{2,3,1,0:T(8,128)(2,1)S(1)} copy(bf16[1,1,512,512]{3,2,1,0:T(8,128)(2,1)} %param.13) | data formatting | bytes 1048576 | tf_op args[1]
  4.0 0.1 compare_convert_fusion
  4.1 1.5 %collective-permute-done.other = bf16[16,8,4096]{2,1,0:T(8,128)(2,1)S(1)} collective-permute-done((bf16[16,8,4096]{2,1,0:T(8,128)(2,1)}, bf16[16,8,4096]{2,1,0:T(8,128)(2,1)S(1)}, u32[]{:S(2)}, u32[]{:S(2)}) %collective-permute-start) | collective-permute-done | bytes 1048608 | tf_op jit(solution)/shard_map/ppermute | solution.py:142
  5.6 0.1 add_pair.2
  5.7 1.3 %collective-permute-start.1 = (bf16[8,512]{1,0:T(8,128)(2,1)S(1)}, bf16[8,512]{1,0:T(8,128)(2,1)S(1)}, u32[]{:S(2)}, u32[]{:S(2)}) collective-permute-start(bf16[8,512]{1,0:T(8,128)(2,1)S(1)} %slice_bitcast_fusion), channel_id=1, source_target_pairs={{64,0},{192,128},{320,256},{448,384},{65,1},{193,129},{321,257},{4... | collective-permute-start | bytes 24584 | tf_op jit(solution)/shard_map/ppermute | solution.py:146
  7.0 0.1 conditional.4
  7.1 14.1 %collective-permute-done.1.refs_0_ = bf16[8,512]{1,0:T(8,128)(2,1)S(1)} collective-permute-done((bf16[8,512]{1,0:T(8,128)(2,1)S(1)}, bf16[8,512]{1,0:T(8,128)(2,1)S(1)}, u32[]{:S(2)}, u32[]{:S(2)}) %collective-permute-start.1) | collective-permute-done | bytes 8224 | tf_op jit(solution)/shard_map/ppermute | solution.py:146
  21.2 0.1 add_pair.3
  21.3 0.0 copy-start.2
  21.3 0.0 copy-start.3
  21.3 0.0 copy-start.4
  21.4 0.0 copy-start.5
  21.4 42.9 %conditional.5 = (bf16[512,512]{1,0:T(8,128)(2,1)S(1)}) conditional(s32[]{:T(128)} %convert_element_type.26, bf16[64,8,512]{2,1,0:T(8,128)(2,1)S(1)} %get-tuple-element.63, (bf16[4,16,8,512]{3,2,1,0:T(8,128)(2,1)S(1)}, bf16[64,16]{0,1:T(8,128)(2,1)S(1)}) %tuple.41), branch_computations={%region_5.6_spmd, %region_6.8_spmd} | conditional | flops 8847360 | bytes 4458506 | solution.py:151
  21.4 10.6 %all_to_all.23 = bf16[4,16,8,512]{3,2,1,0:T(8,128)(2,1)S(1)} all-to-all(bf16[4,16,8,512]{3,2,1,0:T(8,128)(2,1)S(1)} %get-tuple-element.27), channel_id=1, replica_groups={{256,384,0,128},{320,448,64,192},{257,385,1,129},{321,449,65,193},{258,..., dimensions={0} | all-to-all | bytes 1048576 | tf_op jit(solution)/shard_map/cond/branch_1_fun/all_to_all | solution.py:120
  32.0 0.1 reduce_sum.23
  32.1 0.3 fusion.2
  32.4 0.3 copy.24
  32.7 31.5 %all_to_all.24 = bf16[64,8,512]{2,1,0:T(8,128)(2,1)S(1)} all-to-all(bf16[64,8,512]{2,1,0:T(8,128)(2,1)S(1)} %copy.24), channel_id=1, replica_groups={{34,35,32,33,38,39,36,37,42,43,40,41,46,47,44,45,50,51,48,49,54,55,52,5..., dimensions={0} | all-to-all | bytes 1048576 | tf_op jit(solution)/shard_map/cond/branch_1_fun/all_to_all | solution.py:115
  64.3 2.1 %soap_step.1 = (bf16[512,512]{1,0:T(8,128)(2,1)}, bf16[512,512]{1,0:T(8,128)(2,1)}, bf16[512,512]{1,0:T(8,128)(2,1)S(1)}) custom-call(bf16[512,512]{1,0:T(8,128)(2,1)S(1)} %get-tuple-element.44.arrived, bf16[512,512]{1,0:T(8,128)(2,1)S(1)} %bitcast.31, bf16[512,512]{1,0:T(8,128)(2,1)S(1)} %bitcast.32, bf16[512,512]{1,0:T(8,128)(2,1)S(1)} %bitcast.34, ...), custom_call_target="tpu_custom_call" | custom-call | flops 1073741824 | bytes 4718592 | tf_op jit(solution)/shard_map/soap_step/pallas_call | solution.py:100
  66.4 28.5 %all_to_all.25 = bf16[64,8,512]{2,1,0:T(8,128)(2,1)S(1)} all-to-all(bf16[64,8,512]{2,1,0:T(8,128)(2,1)S(1)} %bitcast.33), channel_id=1, replica_groups={{34,35,32,33,38,39,36,37,42,43,40,41,46,47,44,45,50,51,48,49,54,55,52,5..., dimensions={0} | all-to-all | bytes 1048576 | tf_op jit(solution)/shard_map/all_to_all | solution.py:115
  94.9 0.3 convolution_convert_fusion.2
  95.2 0.7 copy.29
  (13 shorter events, 0.1 us)
Async XLA Ops:
  0.6 3.4 %copy-start = (s32[8,16]{1,0:T(8,128)S(1)}, s32[8,16]{1,0:T(8,128)}, u32[]{:S(2)}) copy-start(s32[8,16]{1,0:T(8,128)} %param.17) | copy-start | bytes 1540
  0.6 4.9 %copy-start.1 = (bf16[1,16,8,4096]{3,2,1,0:T(8,128)(2,1)S(1)}, bf16[1,16,8,4096]{3,2,1,0:T(8,128)(2,1)}, u32[]{:S(2)}) copy-start(bf16[1,16,8,4096]{3,2,1,0:T(8,128)(2,1)} %param.12) | copy-start | bytes 3145732
  0.7 4.9 %collective-permute-start = (bf16[16,8,4096]{2,1,0:T(8,128)(2,1)}, bf16[16,8,4096]{2,1,0:T(8,128)(2,1)S(1)}, u32[]{:S(2)}, u32[]{:S(2)}) collective-permute-start(bf16[16,8,4096]{2,1,0:T(8,128)(2,1)} %bitcast.28), channel_id=1, source_target_pairs={{0,64},{64,0},{128,192},{192,128},{256,320},{320,256},{384,448},{4... | collective-permute-start | bytes 3145736 | tf_op jit(solution)/shard_map/ppermute | solution.py:142
  5.7 15.5 %collective-permute-start.1 = (bf16[8,512]{1,0:T(8,128)(2,1)S(1)}, bf16[8,512]{1,0:T(8,128)(2,1)S(1)}, u32[]{:S(2)}, u32[]{:S(2)}) collective-permute-start(bf16[8,512]{1,0:T(8,128)(2,1)S(1)} %slice_bitcast_fusion), channel_id=1, source_target_pairs={{64,0},{192,128},{320,256},{448,384},{65,1},{193,129},{321,257},{4... | collective-permute-start | bytes 24584 | tf_op jit(solution)/shard_map/ppermute | solution.py:146
  21.3 43.0 %copy-start.2 = (bf16[1,1,512,512]{3,2,1,0:T(8,128)(2,1)S(1)}, bf16[1,1,512,512]{3,2,1,0:T(8,128)(2,1)}, u32[]{:S(2)}) copy-start(bf16[1,1,512,512]{3,2,1,0:T(8,128)(2,1)} %param.13) | copy-start | bytes 1572868
  21.3 43.0 %copy-start.3 = (bf16[1,1,512,512]{3,2,1,0:T(8,128)(2,1)S(1)}, bf16[1,1,512,512]{3,2,1,0:T(8,128)(2,1)}, u32[]{:S(2)}) copy-start(bf16[1,1,512,512]{3,2,1,0:T(8,128)(2,1)} %param.14) | copy-start | bytes 1572868
  21.3 42.9 %copy-start.4 = (bf16[1,1,512,512]{3,2,1,0:T(8,128)(2,1)S(1)}, bf16[1,1,512,512]{3,2,1,0:T(8,128)(2,1)}, u32[]{:S(2)}) copy-start(bf16[1,1,512,512]{3,2,1,0:T(8,128)(2,1)} %param.15) | copy-start | bytes 1572868
  21.4 42.9 %copy-start.5 = (bf16[1,1,512,512]{3,2,1,0:T(8,128)(2,1)S(1)}, bf16[1,1,512,512]{3,2,1,0:T(8,128)(2,1)}, u32[]{:S(2)}) copy-start(bf16[1,1,512,512]{3,2,1,0:T(8,128)(2,1)} %param.16) | copy-start | bytes 1572868

commit v9 on v6

--- a/solution.py
+++ b/solution.py
@@ -14,13 +14,16 @@
 BLOCKS = 16
 STRIP = 128
 
-PLANES = [8, 0, 1, 15, 2, 14, 3, 13, 4, 12, 5, 11, 6, 10, 7, 9]
-ORDER = [z * N_Y + (y + N_Y // 2) % N_Y for z in PLANES for y in range(N_Y)]
-PAIR = 2 * SUB
+def natural_of(p):
+    return (p // N_Y + N_Z // 2) % N_Z * N_Y + (p % N_Y + N_Y // 2) % N_Y
 
 
 def chip_of(p):
     return (p + N_X // 2) % N_X
+
+
+ORDER = [natural_of(p) for p in range(N_FSDP)]
+PAIR = 2 * SUB
 
 
 def hbm():
@@ -65,6 +68,7 @@
     turned = jnp.dot(left_turned[...], grad[...], preferred_element_type=jnp.float32).astype(
         jnp.bfloat16
     )
+    stores = []
     for i in range(SIDE // STRIP):
         rows = slice(i * STRIP, (i + 1) * STRIP)
         rotated = jnp.dot(turned[rows], right[...], preferred_element_type=jnp.float32)
@@ -73,12 +77,10 @@
         first_new[rows, :] = one.astype(jnp.bfloat16)
         second_new[rows, :] = two.astype(jnp.bfloat16)
         ratio[rows, :] = (one / (two * lax.rsqrt(two) + 1e-08)).astype(jnp.bfloat16)
-    stores = [
-        pltpu.make_async_copy(first_new, first_new_hbm, sems.at[0]),
-        pltpu.make_async_copy(second_new, second_new_hbm, sems.at[1]),
-    ]
-    for c in stores:
-        c.start()
+        for j, (src, dst) in enumerate(((first_new, first_new_hbm), (second_new, second_new_hbm))):
+            part = pl.ds(i * STRIP, STRIP)
+            stores.append(pltpu.make_async_copy(src.at[part], dst.at[part], sems.at[2 * i + j]))
+            stores[-1].start()
     back = jnp.dot(left[...], ratio[...], preferred_element_type=jnp.float32).astype(jnp.bfloat16)
     block_update = lax.dot_general(
         back, right[...], (((1,), (1,)), ((), ())), preferred_element_type=jnp.float32
@@ -96,7 +98,8 @@
         out_shape=(square, square, square),
         in_specs=[vmem()] * 6,
         out_specs=(hbm(), hbm(), vmem()),
-        scratch_shapes=[pltpu.VMEM((SIDE, SIDE), jnp.bfloat16)] * 4 + [pltpu.SemaphoreType.DMA((2,))],
+        scratch_shapes=[pltpu.VMEM((SIDE, SIDE), jnp.bfloat16)] * 4
+        + [pltpu.SemaphoreType.DMA((2 * SIDE // STRIP,))],
         compiler_params=pltpu.CompilerParams(vmem_limit_bytes=24 * 1024 * 1024),
         cost_estimate=pl.CostEstimate(
             flops=8 * SIDE**3, bytes_accessed=18 * SIDE**2, transcendentals=2 * SIDE**2
@@ -120,7 +123,7 @@
     rep = lax.axis_index("rep")
     core = lax.rem(rep, 2)
     owner_row = lax.dynamic_slice_in_dim(owners, rep, 1, 0)[0]
-    slots = jnp.array(ORDER, jnp.int32)
+    slots = natural_of(jnp.arange(N_FSDP, dtype=jnp.int32))
     selector = (owner_row[None, :] == slots[:, None]).astype(jnp.bfloat16)
     left = left_basis[0, 0]
     right = right_basis[0, 0]

time: 96.5 us -> 96.3 us (level)
    unnamed x16 -> x14, local copies, waits for them, and re-layouts: 2.66 us -> 2.03 us
where the time goes in v9:
time: 96.3 us; the launch traced here: 95.7 us
  blocking collectives  70.7 us (73%)
  waiting for transfers between devices  15.6 us (16%)
  starting transfers between devices  3.34 us (3%)
  local copies, waits for them, and re-layouts  2.39 us (2%)
  Pallas kernels  2.09 us (2%)
    all_to_all x2, blocking collectives, exchange(): lax.all_to_all(pieces, 'fsdp', 0, 0, axis_index_groups=[ORDER], tiled=True)  60.2 us
    ppermute x1, waiting for transfers between devices, local(): lax.ppermute(early[0], 'rep', [(i + 1, i) for i in range(0, n_rep, 2)])  14.2 us
    all_to_all x1, blocking collectives, sum_over_x(): lax.all_to_all(pair, 'rep', 0, 0, axis_index_groups=chips, tiled=True)  10.5 us
    ppermute x1, starting transfers between devices, local(): other = lax.ppermute(own, 'rep', [(i, i ^ 1) for i in range(n_rep)])  2.05 us
    unnamed x14, local copies, waits for them, and re-layouts  2.03 us
  transfers between devices with their start and end apart: 2, of which 2 were waited for; matrix products, arithmetic and copies ran while one was open for 1% of the time, Pallas kernels for 0%

profile of v9, /device:TPU:6, one launch (start us, length us, event | category | flops | bytes accessed | tf_op | source)
XLA Modules:
  0.0 95.7 jit_solution(7551233157153426867)
XLA Ops:
  0.6 0.0 copy-start
  0.7 2.1 %collective-permute-start = (bf16[16,8,4096]{2,1,0:T(8,128)(2,1)}, bf16[16,8,4096]{2,1,0:T(8,128)(2,1)S(1)}, u32[]{:S(2)}, u32[]{:S(2)}) collective-permute-start(bf16[16,8,4096]{2,1,0:T(8,128)(2,1)} %bitcast.22), channel_id=1, source_target_pairs={{0,64},{64,0},{128,192},{192,128},{256,320},{320,256},{384,448},{4... | collective-permute-start | bytes 3145736 | tf_op jit(solution)/shard_map/ppermute | solution.py:132
  2.7 1.3 %copy.15 = bf16[1,1,512,512]{2,3,1,0:T(8,128)(2,1)S(1)} copy(bf16[1,1,512,512]{3,2,1,0:T(8,128)(2,1)} %param.11) | data formatting | bytes 1048576 | tf_op args[1]
  4.0 0.1 compare_convert_fusion
  4.1 1.5 %collective-permute-done.other = bf16[16,8,4096]{2,1,0:T(8,128)(2,1)S(1)} collective-permute-done((bf16[16,8,4096]{2,1,0:T(8,128)(2,1)}, bf16[16,8,4096]{2,1,0:T(8,128)(2,1)S(1)}, u32[]{:S(2)}, u32[]{:S(2)}) %collective-permute-start) | collective-permute-done | bytes 1048608 | tf_op jit(solution)/shard_map/ppermute | solution.py:132
  5.6 0.0 copy-done.1
  5.6 0.1 add_pair.2
  5.7 1.3 %collective-permute-start.1 = (bf16[8,512]{1,0:T(8,128)(2,1)S(1)}, bf16[8,512]{1,0:T(8,128)(2,1)S(1)}, u32[]{:S(2)}, u32[]{:S(2)}) collective-permute-start(bf16[8,512]{1,0:T(8,128)(2,1)S(1)} %slice_bitcast_fusion), channel_id=1, source_target_pairs={{64,0},{192,128},{320,256},{448,384},{65,1},{193,129},{321,257},{4... | collective-permute-start | bytes 24584 | tf_op jit(solution)/shard_map/ppermute | solution.py:136
  7.0 14.2 %collective-permute-done.1.refs_0_ = bf16[8,512]{1,0:T(8,128)(2,1)S(1)} collective-permute-done((bf16[8,512]{1,0:T(8,128)(2,1)S(1)}, bf16[8,512]{1,0:T(8,128)(2,1)S(1)}, u32[]{:S(2)}, u32[]{:S(2)}) %collective-permute-start.1) | collective-permute-done | bytes 8224 | tf_op jit(solution)/shard_map/ppermute | solution.py:136
  21.2 0.1 add_pair.3
  21.3 10.6 %conditional.3 = (bf16[16,8,512]{2,0,1:T(8,128)(2,1)S(1)}) conditional(s32[]{:T(128)} %convert_element_type.20, bf16[16,8,512]{2,1,0:T(8,128)(2,1)S(1)} %get-tuple-element.33, bf16[4,16,8,512]{3,2,1,0:T(8,128)(2,1)S(1)} %add_pair.3), branch_computations={%region_3.4_spmd, %region_4.6_spmd} | conditional | flops 196608 | bytes 1966090 | solution.py:138
  21.3 10.5 %all_to_all.19 = bf16[4,16,8,512]{3,2,1,0:T(8,128)(2,1)S(1)} all-to-all(bf16[4,16,8,512]{3,2,1,0:T(8,128)(2,1)S(1)} %param.3), channel_id=1, replica_groups={{256,384,0,128},{320,448,64,192},{257,385,1,129},{321,449,65,193},{258,..., dimensions={0} | all-to-all | bytes 1048576 | tf_op jit(solution)/shard_map/cond/branch_1_fun/all_to_all | solution.py:117
  31.8 0.1 reduce_sum.23
  32.0 0.3 convolution_convert_fusion
  32.3 0.0 copy-start.4
  32.3 0.0 copy-start.5
  32.3 0.3 copy.17
  32.6 0.0 copy-start.2
  32.6 0.0 copy-start.3
  32.6 31.7 %all_to_all.20 = bf16[64,8,512]{2,1,0:T(8,128)(2,1)S(1)} all-to-all(bf16[64,8,512]{2,1,0:T(8,128)(2,1)S(1)} %copy.17), channel_id=1, replica_groups={{34,35,32,33,38,39,36,37,42,43,40,41,46,47,44,45,50,51,48,49,54,55,52,5..., dimensions={0} | all-to-all | bytes 1048576 | tf_op jit(solution)/shard_map/all_to_all | solution.py:112
  64.3 1.8 %soap_step.1 = (bf16[512,512]{1,0:T(8,128)(2,1)}, bf16[512,512]{1,0:T(8,128)(2,1)}, bf16[512,512]{1,0:T(8,128)(2,1)S(1)}) custom-call(bf16[512,512]{1,0:T(8,128)(2,1)S(1)} %bitcast.27, bf16[512,512]{1,0:T(8,128)(2,1)S(1)} %bitcast.25, bf16[512,512]{1,0:T(8,128)(2,1)S(1)} %bitcast.26, bf16[512,512]{1,0:T(8,128)(2,1)S(1)} %bitcast.29, ...), custom_call_target="tpu_custom_call" | custom-call | flops 1073741824 | bytes 4718592 | tf_op jit(solution)/shard_map/soap_step/pallas_call | solution.py:96
  66.2 28.5 %all_to_all.21 = bf16[64,8,512]{2,1,0:T(8,128)(2,1)S(1)} all-to-all(bf16[64,8,512]{2,1,0:T(8,128)(2,1)S(1)} %bitcast.28), channel_id=1, replica_groups={{34,35,32,33,38,39,36,37,42,43,40,41,46,47,44,45,50,51,48,49,54,55,52,5..., dimensions={0} | all-to-all | bytes 1048576 | tf_op jit(solution)/shard_map/all_to_all | solution.py:112
  94.7 0.3 convolution_convert_fusion.1
  95.0 0.7 copy.20
  (12 shorter events, 0.1 us)
Async XLA Ops:
  0.6 3.4 %copy-start = (s32[8,16]{1,0:T(8,128)S(1)}, s32[8,16]{1,0:T(8,128)}, u32[]{:S(2)}) copy-start(s32[8,16]{1,0:T(8,128)} %param.15) | copy-start | bytes 1540
  0.6 4.9 %copy-start.1 = (bf16[1,16,8,4096]{3,2,1,0:T(8,128)(2,1)S(1)}, bf16[1,16,8,4096]{3,2,1,0:T(8,128)(2,1)}, u32[]{:S(2)}) copy-start(bf16[1,16,8,4096]{3,2,1,0:T(8,128)(2,1)} %param.10) | copy-start | bytes 3145732
  0.7 4.9 %collective-permute-start = (bf16[16,8,4096]{2,1,0:T(8,128)(2,1)}, bf16[16,8,4096]{2,1,0:T(8,128)(2,1)S(1)}, u32[]{:S(2)}, u32[]{:S(2)}) collective-permute-start(bf16[16,8,4096]{2,1,0:T(8,128)(2,1)} %bitcast.22), channel_id=1, source_target_pairs={{0,64},{64,0},{128,192},{192,128},{256,320},{320,256},{384,448},{4... | collective-permute-start | bytes 3145736 | tf_op jit(solution)/shard_map/ppermute | solution.py:132
  5.7 15.5 %collective-permute-start.1 = (bf16[8,512]{1,0:T(8,128)(2,1)S(1)}, bf16[8,512]{1,0:T(8,128)(2,1)S(1)}, u32[]{:S(2)}, u32[]{:S(2)}) collective-permute-start(bf16[8,512]{1,0:T(8,128)(2,1)S(1)} %slice_bitcast_fusion), channel_id=1, source_target_pairs={{64,0},{192,128},{320,256},{448,384},{65,1},{193,129},{321,257},{4... | collective-permute-start | bytes 24584 | tf_op jit(solution)/shard_map/ppermute | solution.py:136
  32.3 32.0 %copy-start.4 = (bf16[1,1,512,512]{3,2,1,0:T(8,128)(2,1)S(1)}, bf16[1,1,512,512]{3,2,1,0:T(8,128)(2,1)}, u32[]{:S(2)}) copy-start(bf16[1,1,512,512]{3,2,1,0:T(8,128)(2,1)} %param.13) | copy-start | bytes 1572868
  32.3 32.0 %copy-start.5 = (bf16[1,1,512,512]{3,2,1,0:T(8,128)(2,1)S(1)}, bf16[1,1,512,512]{3,2,1,0:T(8,128)(2,1)}, u32[]{:S(2)}) copy-start(bf16[1,1,512,512]{3,2,1,0:T(8,128)(2,1)} %param.14) | copy-start | bytes 1572868
  32.6 31.7 %copy-start.2 = (bf16[1,1,512,512]{3,2,1,0:T(8,128)(2,1)S(1)}, bf16[1,1,512,512]{3,2,1,0:T(8,128)(2,1)}, u32[]{:S(2)}) copy-start(bf16[1,1,512,512]{3,2,1,0:T(8,128)(2,1)} %param.11) | copy-start | bytes 1572868
  32.6 31.7 %copy-start.3 = (bf16[1,1,512,512]{3,2,1,0:T(8,128)(2,1)S(1)}, bf16[1,1,512,512]{3,2,1,0:T(8,128)(2,1)}, u32[]{:S(2)}) copy-start(bf16[1,1,512,512]{3,2,1,0:T(8,128)(2,1)} %param.12) | copy-start | bytes 1572868

commit v10 on v9

--- a/solution.py
+++ b/solution.py
@@ -8,6 +8,7 @@
 N_X = 4
 N_Y = 4
 N_Z = 16
+LAST_Z = 10
 N_FSDP = N_Z * N_Y
 SUB = 8
 SIDE = 512
@@ -15,7 +16,7 @@
 STRIP = 128
 
 def natural_of(p):
-    return (p // N_Y + N_Z // 2) % N_Z * N_Y + (p % N_Y + N_Y // 2) % N_Y
+    return (p // N_Y + LAST_Z) % N_Z * N_Y + (p % N_Y + N_Y // 2) % N_Y
 
 
 def chip_of(p):

time: 96.3 us -> 96.2 us (level)
  no operation moved by 1% of the time
where the time goes in v10:
time: 96.2 us; the launch traced here: 95.7 us
  blocking collectives  70.6 us (73%)
  waiting for transfers between devices  15.6 us (16%)
  starting transfers between devices  3.34 us (3%)
  local copies, waits for them, and re-layouts  2.39 us (2%)
  Pallas kernels  2.09 us (2%)
    all_to_all x2, blocking collectives, exchange(): lax.all_to_all(pieces, 'fsdp', 0, 0, axis_index_groups=[ORDER], tiled=True)  60.1 us
    ppermute x1, waiting for transfers between devices, local(): lax.ppermute(early[0], 'rep', [(i + 1, i) for i in range(0, n_rep, 2)])  14.2 us
    all_to_all x1, blocking collectives, sum_over_x(): lax.all_to_all(pair, 'rep', 0, 0, axis_index_groups=chips, tiled=True)  10.5 us
    ppermute x1, starting transfers between devices, local(): other = lax.ppermute(own, 'rep', [(i, i ^ 1) for i in range(n_rep)])  2.05 us
    unnamed x14, local copies, waits for them, and re-layouts  2.03 us
  transfers between devices with their start and end apart: 2, of which 2 were waited for; matrix products, arithmetic and copies ran while one was open for 1% of the time, Pallas kernels for 0%

profile of v10, /device:TPU:6, one launch (start us, length us, event | category | flops | bytes accessed | tf_op | source)
XLA Modules:
  0.0 95.7 jit_solution(10581066226714668400)
XLA Ops:
  0.6 0.0 copy-start
  0.6 0.0 copy-start.1
  0.7 2.1 %collective-permute-start = (bf16[16,8,4096]{2,1,0:T(8,128)(2,1)}, bf16[16,8,4096]{2,1,0:T(8,128)(2,1)S(1)}, u32[]{:S(2)}, u32[]{:S(2)}) collective-permute-start(bf16[16,8,4096]{2,1,0:T(8,128)(2,1)} %bitcast.22), channel_id=1, source_target_pairs={{0,64},{64,0},{128,192},{192,128},{256,320},{320,256},{384,448},{4... | collective-permute-start | bytes 3145736 | tf_op jit(solution)/shard_map/ppermute | solution.py:133
  2.7 1.3 %copy.15 = bf16[1,1,512,512]{2,3,1,0:T(8,128)(2,1)S(1)} copy(bf16[1,1,512,512]{3,2,1,0:T(8,128)(2,1)} %param.11) | data formatting | bytes 1048576 | tf_op args[1]
  4.0 0.1 compare_convert_fusion
  4.1 1.5 %collective-permute-done.other = bf16[16,8,4096]{2,1,0:T(8,128)(2,1)S(1)} collective-permute-done((bf16[16,8,4096]{2,1,0:T(8,128)(2,1)}, bf16[16,8,4096]{2,1,0:T(8,128)(2,1)S(1)}, u32[]{:S(2)}, u32[]{:S(2)}) %collective-permute-start) | collective-permute-done | bytes 1048608 | tf_op jit(solution)/shard_map/ppermute | solution.py:133
  5.6 0.1 add_pair.2
  5.7 1.3 %collective-permute-start.1 = (bf16[8,512]{1,0:T(8,128)(2,1)S(1)}, bf16[8,512]{1,0:T(8,128)(2,1)S(1)}, u32[]{:S(2)}, u32[]{:S(2)}) collective-permute-start(bf16[8,512]{1,0:T(8,128)(2,1)S(1)} %slice_bitcast_fusion), channel_id=1, source_target_pairs={{64,0},{192,128},{320,256},{448,384},{65,1},{193,129},{321,257},{4... | collective-permute-start | bytes 24584 | tf_op jit(solution)/shard_map/ppermute | solution.py:137
  7.0 14.2 %collective-permute-done.1.refs_0_ = bf16[8,512]{1,0:T(8,128)(2,1)S(1)} collective-permute-done((bf16[8,512]{1,0:T(8,128)(2,1)S(1)}, bf16[8,512]{1,0:T(8,128)(2,1)S(1)}, u32[]{:S(2)}, u32[]{:S(2)}) %collective-permute-start.1) | collective-permute-done | bytes 8224 | tf_op jit(solution)/shard_map/ppermute | solution.py:137
  21.2 0.1 add_pair.3
  21.3 10.6 %conditional.3 = (bf16[16,8,512]{2,0,1:T(8,128)(2,1)S(1)}) conditional(s32[]{:T(128)} %convert_element_type.20, bf16[16,8,512]{2,1,0:T(8,128)(2,1)S(1)} %get-tuple-element.33, bf16[4,16,8,512]{3,2,1,0:T(8,128)(2,1)S(1)} %add_pair.3), branch_computations={%region_3.4_spmd, %region_4.6_spmd} | conditional | flops 196608 | bytes 1966090 | solution.py:139
  21.3 10.5 %all_to_all.19 = bf16[4,16,8,512]{3,2,1,0:T(8,128)(2,1)S(1)} all-to-all(bf16[4,16,8,512]{3,2,1,0:T(8,128)(2,1)S(1)} %param.3), channel_id=1, replica_groups={{256,384,0,128},{320,448,64,192},{257,385,1,129},{321,449,65,193},{258,..., dimensions={0} | all-to-all | bytes 1048576 | tf_op jit(solution)/shard_map/cond/branch_1_fun/all_to_all | solution.py:118
  31.8 0.1 reduce_sum.23
  32.0 0.3 convolution_convert_fusion
  32.3 0.0 copy-start.4
  32.3 0.0 copy-start.5
  32.3 0.3 copy.17
  32.6 0.0 copy-start.2
  32.6 0.0 copy-start.3
  32.6 31.5 %all_to_all.20 = bf16[64,8,512]{2,1,0:T(8,128)(2,1)S(1)} all-to-all(bf16[64,8,512]{2,1,0:T(8,128)(2,1)S(1)} %copy.17), channel_id=1, replica_groups={{42,43,40,41,46,47,44,45,50,51,48,49,54,55,52,53,58,59,56,57,62,63,60,6..., dimensions={0} | all-to-all | bytes 1048576 | tf_op jit(solution)/shard_map/all_to_all | solution.py:113
  64.2 1.8 %soap_step.1 = (bf16[512,512]{1,0:T(8,128)(2,1)}, bf16[512,512]{1,0:T(8,128)(2,1)}, bf16[512,512]{1,0:T(8,128)(2,1)S(1)}) custom-call(bf16[512,512]{1,0:T(8,128)(2,1)S(1)} %bitcast.27, bf16[512,512]{1,0:T(8,128)(2,1)S(1)} %bitcast.25, bf16[512,512]{1,0:T(8,128)(2,1)S(1)} %bitcast.26, bf16[512,512]{1,0:T(8,128)(2,1)S(1)} %bitcast.29, ...), custom_call_target="tpu_custom_call" | custom-call | flops 1073741824 | bytes 4718592 | tf_op jit(solution)/shard_map/soap_step/pallas_call | solution.py:97
  66.0 28.6 %all_to_all.21 = bf16[64,8,512]{2,1,0:T(8,128)(2,1)S(1)} all-to-all(bf16[64,8,512]{2,1,0:T(8,128)(2,1)S(1)} %bitcast.28), channel_id=1, replica_groups={{42,43,40,41,46,47,44,45,50,51,48,49,54,55,52,53,58,59,56,57,62,63,60,6..., dimensions={0} | all-to-all | bytes 1048576 | tf_op jit(solution)/shard_map/all_to_all | solution.py:113
  94.6 0.3 convolution_convert_fusion.1
  94.9 0.7 copy.20
  (12 shorter events, 0.1 us)
Async XLA Ops:
  0.6 3.4 %copy-start = (s32[8,16]{1,0:T(8,128)S(1)}, s32[8,16]{1,0:T(8,128)}, u32[]{:S(2)}) copy-start(s32[8,16]{1,0:T(8,128)} %param.15) | copy-start | bytes 1540
  0.6 4.9 %copy-start.1 = (bf16[1,16,8,4096]{3,2,1,0:T(8,128)(2,1)S(1)}, bf16[1,16,8,4096]{3,2,1,0:T(8,128)(2,1)}, u32[]{:S(2)}) copy-start(bf16[1,16,8,4096]{3,2,1,0:T(8,128)(2,1)} %param.10) | copy-start | bytes 3145732
  0.7 4.9 %collective-permute-start = (bf16[16,8,4096]{2,1,0:T(8,128)(2,1)}, bf16[16,8,4096]{2,1,0:T(8,128)(2,1)S(1)}, u32[]{:S(2)}, u32[]{:S(2)}) collective-permute-start(bf16[16,8,4096]{2,1,0:T(8,128)(2,1)} %bitcast.22), channel_id=1, source_target_pairs={{0,64},{64,0},{128,192},{192,128},{256,320},{320,256},{384,448},{4... | collective-permute-start | bytes 3145736 | tf_op jit(solution)/shard_map/ppermute | solution.py:133
  5.7 15.5 %collective-permute-start.1 = (bf16[8,512]{1,0:T(8,128)(2,1)S(1)}, bf16[8,512]{1,0:T(8,128)(2,1)S(1)}, u32[]{:S(2)}, u32[]{:S(2)}) collective-permute-start(bf16[8,512]{1,0:T(8,128)(2,1)S(1)} %slice_bitcast_fusion), channel_id=1, source_target_pairs={{64,0},{192,128},{320,256},{448,384},{65,1},{193,129},{321,257},{4... | collective-permute-start | bytes 24584 | tf_op jit(solution)/shard_map/ppermute | solution.py:137
  32.3 31.9 %copy-start.4 = (bf16[1,1,512,512]{3,2,1,0:T(8,128)(2,1)S(1)}, bf16[1,1,512,512]{3,2,1,0:T(8,128)(2,1)}, u32[]{:S(2)}) copy-start(bf16[1,1,512,512]{3,2,1,0:T(8,128)(2,1)} %param.13) | copy-start | bytes 1572868
  32.3 31.8 %copy-start.5 = (bf16[1,1,512,512]{3,2,1,0:T(8,128)(2,1)S(1)}, bf16[1,1,512,512]{3,2,1,0:T(8,128)(2,1)}, u32[]{:S(2)}) copy-start(bf16[1,1,512,512]{3,2,1,0:T(8,128)(2,1)} %param.14) | copy-start | bytes 1572868
  32.6 31.5 %copy-start.2 = (bf16[1,1,512,512]{3,2,1,0:T(8,128)(2,1)S(1)}, bf16[1,1,512,512]{3,2,1,0:T(8,128)(2,1)}, u32[]{:S(2)}) copy-start(bf16[1,1,512,512]{3,2,1,0:T(8,128)(2,1)} %param.11) | copy-start | bytes 1572868
  32.6 31.5 %copy-start.3 = (bf16[1,1,512,512]{3,2,1,0:T(8,128)(2,1)S(1)}, bf16[1,1,512,512]{3,2,1,0:T(8,128)(2,1)}, u32[]{:S(2)}) copy-start(bf16[1,1,512,512]{3,2,1,0:T(8,128)(2,1)} %param.12) | copy-start | bytes 1572868

commit v11 on v9

--- a/solution.py
+++ b/solution.py
@@ -112,10 +112,9 @@
     return lax.all_to_all(pieces, "fsdp", 0, 0, axis_index_groups=[ORDER], tiled=True)
 
 
-def sum_over_x(pair):
+def exchange_over_x(pair):
     chips = [[2 * chip_of(p) + core for p in range(N_X)] for core in range(2)]
-    parts = lax.all_to_all(pair, "rep", 0, 0, axis_index_groups=chips, tiled=True)
-    return jnp.sum(parts.astype(jnp.float32), axis=0).astype(jnp.bfloat16)
+    return lax.all_to_all(pair, "rep", 0, 0, axis_index_groups=chips, tiled=True)
 
 
 def local(partials, left_basis, right_basis, first_moment, second_moment, owners):
@@ -132,13 +131,16 @@
     other = lax.ppermute(own, "rep", [(i, i ^ 1) for i in range(n_rep)])
     other, left_turned, selector = lax.optimization_barrier((other, left.T, selector))
     pair = add_pair(own, other)
-    early = lax.cond(core == 1, sum_over_x, lambda p: jnp.zeros(p.shape[1:], p.dtype), pair)
-    follow = lax.ppermute(early[0], "rep", [(i + 1, i) for i in range(0, n_rep, 2)])
+    early = lax.cond(core == 1, exchange_over_x, jnp.zeros_like, pair)
+    follow = lax.ppermute(early[0, 0], "rep", [(i + 1, i) for i in range(0, n_rep, 2)])
     pair = add_pair(own, other, follow)
-    pieces = lax.cond(core == 0, lambda p, e: sum_over_x(p), lambda p, e: e, pair, early)
+    terms = lax.cond(core == 0, lambda p, e: exchange_over_x(p), lambda p, e: e, pair, early)
 
     outgoing = jnp.einsum(
-        "qb,bsk->qsk", selector, pieces, preferred_element_type=jnp.float32
+        "qt,tsk->qsk",
+        jnp.tile(selector, (1, N_X)),
+        terms.reshape(N_X * BLOCKS, SUB, SIDE),
+        preferred_element_type=jnp.float32,
     ).astype(jnp.bfloat16)
     arrived = exchange(outgoing)
     first_new, second_new, leaving = step(

time: 96.3 us -> 98.1 us (1.019)
  no operation moved by 1% of the time
where the time goes in v11:
time: 98.1 us; the launch traced here: 97.5 us
  blocking collectives  71.5 us (73%)
  waiting for transfers between devices  15.7 us (16%)
  starting transfers between devices  3.34 us (3%)
  Pallas kernels  2.88 us (3%)
  local copies, waits for them, and re-layouts  2.53 us (3%)
    all_to_all x2, blocking collectives, exchange(): lax.all_to_all(pieces, 'fsdp', 0, 0, axis_index_groups=[ORDER], tiled=True)  61 us
    ppermute x1, waiting for transfers between devices, local(): lax.ppermute(early[0, 0], 'rep', [(i + 1, i) for i in range(0, n_rep, 2)])  14.2 us
    all_to_all x1, blocking collectives, exchange_over_x(): lax.all_to_all(pair, 'rep', 0, 0, axis_index_groups=chips, tiled=True)  10.5 us
    ppermute x1, starting transfers between devices, local(): other = lax.ppermute(own, 'rep', [(i, i ^ 1) for i in range(n_rep)])  2.05 us
    unnamed x14, local copies, waits for them, and re-layouts  2.03 us
  transfers between devices with their start and end apart: 2, of which 2 were waited for; matrix products, arithmetic and copies ran while one was open for 1% of the time, Pallas kernels for 0%

profile of v11, /device:TPU:6, one launch (start us, length us, event | category | flops | bytes accessed | tf_op | source)
XLA Modules:
  0.0 97.5 jit_solution(16613636359929128720)
XLA Ops:
  0.6 0.0 copy-start
  0.7 2.1 %collective-permute-start = (bf16[16,8,4096]{2,1,0:T(8,128)(2,1)}, bf16[16,8,4096]{2,1,0:T(8,128)(2,1)S(1)}, u32[]{:S(2)}, u32[]{:S(2)}) collective-permute-start(bf16[16,8,4096]{2,1,0:T(8,128)(2,1)} %bitcast.25), channel_id=1, source_target_pairs={{0,64},{64,0},{128,192},{192,128},{256,320},{320,256},{384,448},{4... | collective-permute-start | bytes 3145736 | tf_op jit(solution)/shard_map/ppermute | solution.py:131
  2.7 1.3 %copy.15 = bf16[1,1,512,512]{2,3,1,0:T(8,128)(2,1)S(1)} copy(bf16[1,1,512,512]{3,2,1,0:T(8,128)(2,1)} %param.11) | data formatting | bytes 1048576 | tf_op args[1]
  4.0 0.1 compare_convert_fusion
  4.1 1.5 %collective-permute-done.other = bf16[16,8,4096]{2,1,0:T(8,128)(2,1)S(1)} collective-permute-done((bf16[16,8,4096]{2,1,0:T(8,128)(2,1)}, bf16[16,8,4096]{2,1,0:T(8,128)(2,1)S(1)}, u32[]{:S(2)}, u32[]{:S(2)}) %collective-permute-start) | collective-permute-done | bytes 1048608 | tf_op jit(solution)/shard_map/ppermute | solution.py:131
  5.6 0.0 copy-done.1
  5.6 0.9 add_pair.2
  6.5 1.3 %collective-permute-start.1 = (bf16[8,512]{1,0:T(8,128)(2,1)S(1)}, bf16[8,512]{1,0:T(8,128)(2,1)S(1)}, u32[]{:S(2)}, u32[]{:S(2)}) collective-permute-start(bf16[8,512]{1,0:T(8,128)(2,1)S(1)} %slice_bitcast_fusion), channel_id=1, source_target_pairs={{64,0},{192,128},{320,256},{448,384},{65,1},{193,129},{321,257},{4... | collective-permute-start | bytes 24584 | tf_op jit(solution)/shard_map/ppermute | solution.py:135
  7.8 14.2 %collective-permute-done.1.refs_0_ = bf16[8,512]{1,0:T(8,128)(2,1)S(1)} collective-permute-done((bf16[8,512]{1,0:T(8,128)(2,1)S(1)}, bf16[8,512]{1,0:T(8,128)(2,1)S(1)}, u32[]{:S(2)}, u32[]{:S(2)}) %collective-permute-start.1) | collective-permute-done | bytes 8224 | tf_op jit(solution)/shard_map/ppermute | solution.py:135
  22.1 0.1 add_pair.3
  22.2 10.7 %conditional.3 = (bf16[4,16,8,512]{3,1,0,2:T(8,128)(2,1)S(1)}) conditional(s32[]{:T(128)} %convert_element_type.16, bf16[4,16,8,512]{3,2,1,0:T(8,128)(2,1)S(1)} %get-tuple-element.36, bf16[4,16,8,512]{3,2,1,0:T(8,128)(2,1)S(1)} %add_pair.3), branch_computations={%region_2.3_spmd, %region_3.4_spmd} | conditional | bytes 2097160 | solution.py:137
  22.2 10.5 %all_to_all.19 = bf16[4,16,8,512]{3,2,1,0:T(8,128)(2,1)S(1)} all-to-all(bf16[4,16,8,512]{3,2,1,0:T(8,128)(2,1)S(1)} %param.3), channel_id=1, replica_groups={{256,384,0,128},{320,448,64,192},{257,385,1,129},{321,449,65,193},{258,..., dimensions={0} | all-to-all | bytes 1048576 | tf_op jit(solution)/shard_map/cond/branch_1_fun/all_to_all | solution.py:117
  32.7 0.2 copy.24
  32.9 0.3 fusion
  33.2 0.0 copy-start.4
  33.2 0.0 copy-start.5
  33.2 0.3 copy.17
  33.5 0.0 copy-start.2
  33.5 0.0 copy-start.3
  33.5 32.5 %all_to_all.20 = bf16[64,8,512]{2,1,0:T(8,128)(2,1)S(1)} all-to-all(bf16[64,8,512]{2,1,0:T(8,128)(2,1)S(1)} %copy.17), channel_id=1, replica_groups={{34,35,32,33,38,39,36,37,42,43,40,41,46,47,44,45,50,51,48,49,54,55,52,5..., dimensions={0} | all-to-all | bytes 1048576 | tf_op jit(solution)/shard_map/all_to_all | solution.py:112
  66.1 1.8 %soap_step.1 = (bf16[512,512]{1,0:T(8,128)(2,1)}, bf16[512,512]{1,0:T(8,128)(2,1)}, bf16[512,512]{1,0:T(8,128)(2,1)S(1)}) custom-call(bf16[512,512]{1,0:T(8,128)(2,1)S(1)} %bitcast.30, bf16[512,512]{1,0:T(8,128)(2,1)S(1)} %bitcast.28, bf16[512,512]{1,0:T(8,128)(2,1)S(1)} %bitcast.29, bf16[512,512]{1,0:T(8,128)(2,1)S(1)} %bitcast.32, ...), custom_call_target="tpu_custom_call" | custom-call | flops 1073741824 | bytes 4718592 | tf_op jit(solution)/shard_map/soap_step/pallas_call | solution.py:96
  67.9 28.5 %all_to_all.21 = bf16[64,8,512]{2,1,0:T(8,128)(2,1)S(1)} all-to-all(bf16[64,8,512]{2,1,0:T(8,128)(2,1)S(1)} %bitcast.31), channel_id=1, replica_groups={{34,35,32,33,38,39,36,37,42,43,40,41,46,47,44,45,50,51,48,49,54,55,52,5..., dimensions={0} | all-to-all | bytes 1048576 | tf_op jit(solution)/shard_map/all_to_all | solution.py:112
  96.4 0.3 convolution_convert_fusion
  96.7 0.7 copy.20
  (11 shorter events, 0.1 us)
Async XLA Ops:
  0.6 3.4 %copy-start = (s32[8,16]{1,0:T(8,128)S(1)}, s32[8,16]{1,0:T(8,128)}, u32[]{:S(2)}) copy-start(s32[8,16]{1,0:T(8,128)} %param.15) | copy-start | bytes 1540
  0.6 4.9 %copy-start.1 = (bf16[1,16,8,4096]{3,2,1,0:T(8,128)(2,1)S(1)}, bf16[1,16,8,4096]{3,2,1,0:T(8,128)(2,1)}, u32[]{:S(2)}) copy-start(bf16[1,16,8,4096]{3,2,1,0:T(8,128)(2,1)} %param.10) | copy-start | bytes 3145732
  0.7 4.9 %collective-permute-start = (bf16[16,8,4096]{2,1,0:T(8,128)(2,1)}, bf16[16,8,4096]{2,1,0:T(8,128)(2,1)S(1)}, u32[]{:S(2)}, u32[]{:S(2)}) collective-permute-start(bf16[16,8,4096]{2,1,0:T(8,128)(2,1)} %bitcast.25), channel_id=1, source_target_pairs={{0,64},{64,0},{128,192},{192,128},{256,320},{320,256},{384,448},{4... | collective-permute-start | bytes 3145736 | tf_op jit(solution)/shard_map/ppermute | solution.py:131
  6.5 15.5 %collective-permute-start.1 = (bf16[8,512]{1,0:T(8,128)(2,1)S(1)}, bf16[8,512]{1,0:T(8,128)(2,1)S(1)}, u32[]{:S(2)}, u32[]{:S(2)}) collective-permute-start(bf16[8,512]{1,0:T(8,128)(2,1)S(1)} %slice_bitcast_fusion), channel_id=1, source_target_pairs={{64,0},{192,128},{320,256},{448,384},{65,1},{193,129},{321,257},{4... | collective-permute-start | bytes 24584 | tf_op jit(solution)/shard_map/ppermute | solution.py:135
  33.2 32.9 %copy-start.4 = (bf16[1,1,512,512]{3,2,1,0:T(8,128)(2,1)S(1)}, bf16[1,1,512,512]{3,2,1,0:T(8,128)(2,1)}, u32[]{:S(2)}) copy-start(bf16[1,1,512,512]{3,2,1,0:T(8,128)(2,1)} %param.13) | copy-start | bytes 1572868
  33.2 32.9 %copy-start.5 = (bf16[1,1,512,512]{3,2,1,0:T(8,128)(2,1)S(1)}, bf16[1,1,512,512]{3,2,1,0:T(8,128)(2,1)}, u32[]{:S(2)}) copy-start(bf16[1,1,512,512]{3,2,1,0:T(8,128)(2,1)} %param.14) | copy-start | bytes 1572868
  33.5 32.5 %copy-start.2 = (bf16[1,1,512,512]{3,2,1,0:T(8,128)(2,1)S(1)}, bf16[1,1,512,512]{3,2,1,0:T(8,128)(2,1)}, u32[]{:S(2)}) copy-start(bf16[1,1,512,512]{3,2,1,0:T(8,128)(2,1)} %param.11) | copy-start | bytes 1572868
  33.5 32.5 %copy-start.3 = (bf16[1,1,512,512]{3,2,1,0:T(8,128)(2,1)S(1)}, bf16[1,1,512,512]{3,2,1,0:T(8,128)(2,1)}, u32[]{:S(2)}) copy-start(bf16[1,1,512,512]{3,2,1,0:T(8,128)(2,1)} %param.12) | copy-start | bytes 1572868

commit v12 on v9

--- a/solution.py
+++ b/solution.py
@@ -81,12 +81,18 @@
             part = pl.ds(i * STRIP, STRIP)
             stores.append(pltpu.make_async_copy(src.at[part], dst.at[part], sems.at[2 * i + j]))
             stores[-1].start()
-    back = jnp.dot(left[...], ratio[...], preferred_element_type=jnp.float32).astype(jnp.bfloat16)
-    block_update = lax.dot_general(
-        back, right[...], (((1,), (1,)), ((), ())), preferred_element_type=jnp.float32
-    ).astype(jnp.bfloat16)
-    for here, natural in places:
-        leaving[here, :] = block_update[natural, :]
+    for low in range(0, SIDE, SIDE // 2):
+        high = low + SIDE // 2
+        back = jnp.dot(left[low:high, :], ratio[...], preferred_element_type=jnp.float32)
+        block_update = lax.dot_general(
+            back.astype(jnp.bfloat16),
+            right[...],
+            (((1,), (1,)), ((), ())),
+            preferred_element_type=jnp.float32,
+        ).astype(jnp.bfloat16)
+        for here, natural in places:
+            if low <= natural.start < high:
+                leaving[here, :] = block_update[natural.start - low : natural.stop - low]
     for c in stores:
         c.wait()
 

time: 96.3 us -> 96.4 us (level)
  no operation moved by 1% of the time
where the time goes in v12:
time: 96.4 us; the launch traced here: 95.8 us
  blocking collectives  70.7 us (73%)
  waiting for transfers between devices  15.6 us (16%)
  starting transfers between devices  3.34 us (3%)
  local copies, waits for them, and re-layouts  2.39 us (2%)
  Pallas kernels  2.15 us (2%)
    all_to_all x2, blocking collectives, exchange(): lax.all_to_all(pieces, 'fsdp', 0, 0, axis_index_groups=[ORDER], tiled=True)  60.2 us
    ppermute x1, waiting for transfers between devices, local(): lax.ppermute(early[0], 'rep', [(i + 1, i) for i in range(0, n_rep, 2)])  14.2 us
    all_to_all x1, blocking collectives, sum_over_x(): lax.all_to_all(pair, 'rep', 0, 0, axis_index_groups=chips, tiled=True)  10.5 us
    ppermute x1, starting transfers between devices, local(): other = lax.ppermute(own, 'rep', [(i, i ^ 1) for i in range(n_rep)])  2.05 us
    unnamed x14, local copies, waits for them, and re-layouts  2.03 us
  transfers between devices with their start and end apart: 2, of which 2 were waited for; matrix products, arithmetic and copies ran while one was open for 1% of the time, Pallas kernels for 0%

profile of v12, /device:TPU:6, one launch (start us, length us, event | category | flops | bytes accessed | tf_op | source)
XLA Modules:
  0.0 95.8 jit_solution(995412641755244438)
XLA Ops:
  0.6 0.0 copy-start
  0.7 2.1 %collective-permute-start = (bf16[16,8,4096]{2,1,0:T(8,128)(2,1)}, bf16[16,8,4096]{2,1,0:T(8,128)(2,1)S(1)}, u32[]{:S(2)}, u32[]{:S(2)}) collective-permute-start(bf16[16,8,4096]{2,1,0:T(8,128)(2,1)} %bitcast.22), channel_id=1, source_target_pairs={{0,64},{64,0},{128,192},{192,128},{256,320},{320,256},{384,448},{4... | collective-permute-start | bytes 3145736 | tf_op jit(solution)/shard_map/ppermute | solution.py:138
  2.7 1.3 %copy.15 = bf16[1,1,512,512]{2,3,1,0:T(8,128)(2,1)S(1)} copy(bf16[1,1,512,512]{3,2,1,0:T(8,128)(2,1)} %param.11) | data formatting | bytes 1048576 | tf_op args[1]
  4.0 0.1 compare_convert_fusion
  4.1 1.5 %collective-permute-done.other = bf16[16,8,4096]{2,1,0:T(8,128)(2,1)S(1)} collective-permute-done((bf16[16,8,4096]{2,1,0:T(8,128)(2,1)}, bf16[16,8,4096]{2,1,0:T(8,128)(2,1)S(1)}, u32[]{:S(2)}, u32[]{:S(2)}) %collective-permute-start) | collective-permute-done | bytes 1048608 | tf_op jit(solution)/shard_map/ppermute | solution.py:138
  5.6 0.1 add_pair.2
  5.7 1.3 %collective-permute-start.1 = (bf16[8,512]{1,0:T(8,128)(2,1)S(1)}, bf16[8,512]{1,0:T(8,128)(2,1)S(1)}, u32[]{:S(2)}, u32[]{:S(2)}) collective-permute-start(bf16[8,512]{1,0:T(8,128)(2,1)S(1)} %slice_bitcast_fusion), channel_id=1, source_target_pairs={{64,0},{192,128},{320,256},{448,384},{65,1},{193,129},{321,257},{4... | collective-permute-start | bytes 24584 | tf_op jit(solution)/shard_map/ppermute | solution.py:142
  7.0 14.2 %collective-permute-done.1.refs_0_ = bf16[8,512]{1,0:T(8,128)(2,1)S(1)} collective-permute-done((bf16[8,512]{1,0:T(8,128)(2,1)S(1)}, bf16[8,512]{1,0:T(8,128)(2,1)S(1)}, u32[]{:S(2)}, u32[]{:S(2)}) %collective-permute-start.1) | collective-permute-done | bytes 8224 | tf_op jit(solution)/shard_map/ppermute | solution.py:142
  21.2 0.1 add_pair.3
  21.3 10.6 %conditional.3 = (bf16[16,8,512]{2,0,1:T(8,128)(2,1)S(1)}) conditional(s32[]{:T(128)} %convert_element_type.20, bf16[16,8,512]{2,1,0:T(8,128)(2,1)S(1)} %get-tuple-element.33, bf16[4,16,8,512]{3,2,1,0:T(8,128)(2,1)S(1)} %add_pair.3), branch_computations={%region_3.4_spmd, %region_4.6_spmd} | conditional | flops 196608 | bytes 1966090 | solution.py:144
  21.3 10.5 %all_to_all.19 = bf16[4,16,8,512]{3,2,1,0:T(8,128)(2,1)S(1)} all-to-all(bf16[4,16,8,512]{3,2,1,0:T(8,128)(2,1)S(1)} %param.3), channel_id=1, replica_groups={{256,384,0,128},{320,448,64,192},{257,385,1,129},{321,449,65,193},{258,..., dimensions={0} | all-to-all | bytes 1048576 | tf_op jit(solution)/shard_map/cond/branch_1_fun/all_to_all | solution.py:123
  31.8 0.1 reduce_sum.23
  32.0 0.3 convolution_convert_fusion
  32.3 0.0 copy-start.4
  32.3 0.0 copy-start.5
  32.3 0.3 copy.17
  32.6 0.0 copy-start.2
  32.6 0.0 copy-start.3
  32.6 31.7 %all_to_all.20 = bf16[64,8,512]{2,1,0:T(8,128)(2,1)S(1)} all-to-all(bf16[64,8,512]{2,1,0:T(8,128)(2,1)S(1)} %copy.17), channel_id=1, replica_groups={{34,35,32,33,38,39,36,37,42,43,40,41,46,47,44,45,50,51,48,49,54,55,52,5..., dimensions={0} | all-to-all | bytes 1048576 | tf_op jit(solution)/shard_map/all_to_all | solution.py:118
  64.3 0.0 copy-done.5
  64.3 1.9 %soap_step.1 = (bf16[512,512]{1,0:T(8,128)(2,1)}, bf16[512,512]{1,0:T(8,128)(2,1)}, bf16[512,512]{1,0:T(8,128)(2,1)S(1)}) custom-call(bf16[512,512]{1,0:T(8,128)(2,1)S(1)} %bitcast.27, bf16[512,512]{1,0:T(8,128)(2,1)S(1)} %bitcast.25, bf16[512,512]{1,0:T(8,128)(2,1)S(1)} %bitcast.26, bf16[512,512]{1,0:T(8,128)(2,1)S(1)} %bitcast.29, ...), custom_call_target="tpu_custom_call" | custom-call | flops 1073741824 | bytes 4718592 | tf_op jit(solution)/shard_map/soap_step/pallas_call | solution.py:102
  66.2 28.5 %all_to_all.21 = bf16[64,8,512]{2,1,0:T(8,128)(2,1)S(1)} all-to-all(bf16[64,8,512]{2,1,0:T(8,128)(2,1)S(1)} %bitcast.28), channel_id=1, replica_groups={{34,35,32,33,38,39,36,37,42,43,40,41,46,47,44,45,50,51,48,49,54,55,52,5..., dimensions={0} | all-to-all | bytes 1048576 | tf_op jit(solution)/shard_map/all_to_all | solution.py:118
  94.8 0.3 convolution_convert_fusion.1
  95.1 0.7 copy.20
  (12 shorter events, 0.1 us)
Async XLA Ops:
  0.6 3.4 %copy-start = (s32[8,16]{1,0:T(8,128)S(1)}, s32[8,16]{1,0:T(8,128)}, u32[]{:S(2)}) copy-start(s32[8,16]{1,0:T(8,128)} %param.15) | copy-start | bytes 1540
  0.6 4.9 %copy-start.1 = (bf16[1,16,8,4096]{3,2,1,0:T(8,128)(2,1)S(1)}, bf16[1,16,8,4096]{3,2,1,0:T(8,128)(2,1)}, u32[]{:S(2)}) copy-start(bf16[1,16,8,4096]{3,2,1,0:T(8,128)(2,1)} %param.10) | copy-start | bytes 3145732
  0.7 4.9 %collective-permute-start = (bf16[16,8,4096]{2,1,0:T(8,128)(2,1)}, bf16[16,8,4096]{2,1,0:T(8,128)(2,1)S(1)}, u32[]{:S(2)}, u32[]{:S(2)}) collective-permute-start(bf16[16,8,4096]{2,1,0:T(8,128)(2,1)} %bitcast.22), channel_id=1, source_target_pairs={{0,64},{64,0},{128,192},{192,128},{256,320},{320,256},{384,448},{4... | collective-permute-start | bytes 3145736 | tf_op jit(solution)/shard_map/ppermute | solution.py:138
  5.7 15.5 %collective-permute-start.1 = (bf16[8,512]{1,0:T(8,128)(2,1)S(1)}, bf16[8,512]{1,0:T(8,128)(2,1)S(1)}, u32[]{:S(2)}, u32[]{:S(2)}) collective-permute-start(bf16[8,512]{1,0:T(8,128)(2,1)S(1)} %slice_bitcast_fusion), channel_id=1, source_target_pairs={{64,0},{192,128},{320,256},{448,384},{65,1},{193,129},{321,257},{4... | collective-permute-start | bytes 24584 | tf_op jit(solution)/shard_map/ppermute | solution.py:142
  32.3 32.0 %copy-start.4 = (bf16[1,1,512,512]{3,2,1,0:T(8,128)(2,1)S(1)}, bf16[1,1,512,512]{3,2,1,0:T(8,128)(2,1)}, u32[]{:S(2)}) copy-start(bf16[1,1,512,512]{3,2,1,0:T(8,128)(2,1)} %param.13) | copy-start | bytes 1572868
  32.3 32.0 %copy-start.5 = (bf16[1,1,512,512]{3,2,1,0:T(8,128)(2,1)S(1)}, bf16[1,1,512,512]{3,2,1,0:T(8,128)(2,1)}, u32[]{:S(2)}) copy-start(bf16[1,1,512,512]{3,2,1,0:T(8,128)(2,1)} %param.14) | copy-start | bytes 1572868
  32.6 31.7 %copy-start.2 = (bf16[1,1,512,512]{3,2,1,0:T(8,128)(2,1)S(1)}, bf16[1,1,512,512]{3,2,1,0:T(8,128)(2,1)}, u32[]{:S(2)}) copy-start(bf16[1,1,512,512]{3,2,1,0:T(8,128)(2,1)} %param.11) | copy-start | bytes 1572868
  32.6 31.7 %copy-start.3 = (bf16[1,1,512,512]{3,2,1,0:T(8,128)(2,1)S(1)}, bf16[1,1,512,512]{3,2,1,0:T(8,128)(2,1)}, u32[]{:S(2)}) copy-start(bf16[1,1,512,512]{3,2,1,0:T(8,128)(2,1)} %param.12) | copy-start | bytes 1572868
